TPU v7x, 128 devices: a whole 4x4x4 slice. The times are simulated.
128 devices in a mesh: row: 8 (over z, core), col: 16 (over y, x).
Axes of the slice: x: 4, y: 4, z: 4, core: 2. Of those that a mesh axis runs over, the one named last changes fastest.
Arguments:
- rhs_held: float32 [393216, 64], P(('row', 'col')), may hold values from -6 to 6
- row_map: int32 [393216], P(('row', 'col')), may hold values from 0 to 393215, as said below
- sep_rhs: float32 [128, 256, 64], P(('row', 'col')), may hold values from -6 to 6
- sep_inverse: float32 [128, 256, 256], P(('row', 'col')), as said below
- sep_parent: float32 [128, 256, 256], P(('row', 'col')), may hold values from -0.1875 to 0.1875
- leaf_inverse: float32 [128, 12, 256, 256], P(('row', 'col')), as said below
- leaf_coupling: float32 [128, 12, 4, 256, 256], P(('row', 'col')), may hold values from -0.1875 to 0.1875
- leaf_links: int32 [128, 12, 4], P(('row', 'col')), may hold values from 0 to 6, as said below
Outputs:
- x_held: float32 [393216, 64], P(('row', 'col'))
- sep_solution: float32 [128, 256, 64], P(('row', 'col'))
Inputs may be any that keep to these rules, and one draw needn't show every extreme that they name: `row_map`: a permutation of all leaf rows; every device holds exactly 24 rows of each device's leaf unknowns. `leaf_links`: the 4 entries of one leaf supernode differ; the first leaf supernode of every device couples to the root, distance 7 - 1. `sep_inverse`: upper triangular, diagonal entries positive. `leaf_inverse`: upper triangular, diagonal entries positive.
All inputs are finite; a program needn't handle non-finite values.
Results may differ from a plain program's by a relative error of at most 0.0003.
Values sent between devices are 32-bit elements; how exact they have to be, the bound alone decides.
A program may use at most 128 MiB of HBM per device.

v0:
```python
import jax
import jax.numpy as jnp
from jax import lax
from jax.sharding import PartitionSpec as P


def regroup_rows(payload, labels, site_flag):
    if site_flag:
        return (
            lax.all_to_all(payload, ("row", "col"), split_axis=0, concat_axis=0, tiled=True),
            lax.all_to_all(labels, ("row", "col"), split_axis=0, concat_axis=0, tiled=True),
        )
    return (
        lax.all_to_all(payload, ("row", "col"), split_axis=0, concat_axis=0, tiled=True),
        labels,
    )


def per_device(
    rhs_held, row_map, sep_rhs, sep_inverse, sep_parent, leaf_inverse, leaf_coupling, leaf_links
):
    devices = lax.axis_size(("row", "col"))
    levels = devices.bit_length() - 1
    device = lax.axis_index(("row", "col"))
    rows_dev, columns = rhs_held.shape
    block_width = sep_rhs.shape[1]
    segment = rows_dev // devices
    by_label = jnp.argsort(row_map)
    send_rows = rhs_held[by_label].reshape(devices, segment, columns)
    send_tags = row_map[by_label].reshape(devices, segment)
    got_rows, got_tags = regroup_rows(send_rows, send_tags, True)
    local_rows = got_tags.reshape(rows_dev) - device * rows_dev
    placement = jnp.argsort(local_rows)
    leaf_rhs = got_rows.reshape(rows_dev, columns)[placement].reshape(-1, block_width, columns)
    empty = jnp.zeros((block_width, columns), jnp.float32)
    sep_out = empty
    ancestors = []
    parent_x = empty
    for level_index in range(levels):
        depth = levels - 1 - level_index
        span = 2 ** (depth + 1)
        owner_id = device // span * span + (2**depth - 1)
        is_owner = device == owner_id

        def solve_own():
            target = sep_rhs[0]
            if level_index > 0:
                target = target - jnp.einsum(
                    "wv,wr->vr", sep_parent[0], parent_x, precision=lax.Precision.HIGHEST
                )
            return jnp.dot(sep_inverse[0], target, precision=lax.Precision.HIGHEST)

        own_value = lax.cond(is_owner, solve_own, lambda: empty)
        sep_out = jnp.where(is_owner, own_value, sep_out)
        slot_index = device // span
        level_slots = jnp.zeros((2**level_index, block_width, columns), jnp.float32)
        level_slots = lax.dynamic_update_slice(level_slots, own_value[None], (slot_index, 0, 0))
        summed = lax.psum(level_slots, ("row", "col"))
        current = lax.dynamic_index_in_dim(summed, slot_index, 0, keepdims=False)
        ancestors.append(current)
        parent_x = current
    reach = leaf_links.max() * 0 + levels
    nearest = jnp.stack([ancestors[levels - 1 - p] for p in range(levels)], axis=0)
    onehot = (leaf_links[0][..., None] == jnp.arange(reach.shape and levels or levels)).astype(
        jnp.float32
    )
    picked = jnp.einsum("scp,pwr->scwr", onehot, nearest, precision=lax.Precision.HIGHEST)
    contrib = jnp.einsum(
        "scwv,scwr->svr", leaf_coupling[0], picked, precision=lax.Precision.HIGHEST
    )
    leaf_x = jnp.einsum(
        "svw,swr->svr", leaf_inverse[0], leaf_rhs - contrib, precision=lax.Precision.HIGHEST
    )
    leaf_flat = leaf_x.reshape(rows_dev, columns)
    send_back = leaf_flat[local_rows].reshape(devices, segment, columns)
    came_back, unused_tags = regroup_rows(send_back, send_tags, False)
    restore = jnp.argsort(by_label)
    x_held = came_back.reshape(rows_dev, columns)[restore]
    return (x_held, sep_out[None])


def solution(mesh):
    in_specs = (
        P(("row", "col"), None),
        P(("row", "col")),
        P(("row", "col"), None, None),
        P(("row", "col"), None, None),
        P(("row", "col"), None, None),
        P(("row", "col"), None, None, None),
        P(("row", "col"), None, None, None, None),
        P(("row", "col"), None, None),
    )
    out_specs = (P(("row", "col"), None), P(("row", "col"), None, None))
    return jax.shard_map(
        per_device, mesh=mesh, in_specs=in_specs, out_specs=out_specs, check_vma=False
    )
```

profile of v0, /device:TPU:1, one launch (start us, length us, event | category | flops | bytes accessed | tf_op | source)
XLA Modules:
  0.0 1173.5 jit_solution(16450042662791751656)
XLA Ops:
  8.1 146.3 %all-reduce.8.cloned.1.call-done = f32[1,256,64]{1,0,2:T(1,128)} async-done(((f32[1,256,64]{1,0,2:T(1,128)}), f32[1,256,64]{1,0,2:T(1,128)}) %all-reduce.8.cloned.1.call-update) | async-done | bytes 65552 | tf_op jit(solution)/shard_map/psum | solution.py:58
  156.8 141.0 %all-reduce.10.cloned.1.call-done = f32[2,256,64]{1,0,2:T(2,128)} async-done(((f32[2,256,64]{1,0,2:T(2,128)}), f32[2,256,64]{1,0,2:T(2,128)}) %all-reduce.10.cloned.1.call-update) | async-done | bytes 131088 | tf_op jit(solution)/shard_map/psum | solution.py:58
  297.8 1.6 constant_dynamic-slice_fusion.5
  301.8 143.3 %all-reduce.12.cloned.1.call-done = f32[4,256,64]{1,0,2:T(4,128)} async-done(((f32[4,256,64]{1,0,2:T(4,128)}), f32[4,256,64]{1,0,2:T(4,128)}) %all-reduce.12.cloned.1.call-update) | async-done | bytes 262160 | tf_op jit(solution)/shard_map/psum | solution.py:58
  445.1 1.6 constant_dynamic-slice_fusion.4
  448.2 2.4 dynamic_update_slice.21
  450.7 146.2 %all-reduce.14.cloned.1.call-done = f32[8,256,64]{1,0,2:T(8,128)} async-done(((f32[8,256,64]{1,0,2:T(8,128)}), f32[8,256,64]{1,0,2:T(8,128)}) %all-reduce.14.cloned.1.call-update) | async-done | bytes 524304 | tf_op jit(solution)/shard_map/psum | solution.py:58
  596.9 1.7 constant_dynamic-slice_fusion.3
  601.0 2.4 dynamic_update_slice.22
  603.5 150.4 %all-reduce.16.cloned.1.call-done = f32[16,256,64]{1,0,2:T(8,128)} async-done(((f32[16,256,64]{1,0,2:T(8,128)}), f32[16,256,64]{1,0,2:T(8,128)}) %all-reduce.16.cloned.1.call-update) | async-done | bytes 1048592 | tf_op jit(solution)/shard_map/psum | solution.py:58
  753.9 1.7 constant_dynamic-slice_fusion.2
  756.9 1.6 broadcast_in_dim.106
  758.5 2.4 dynamic_update_slice.23
  761.0 151.8 %all-reduce.18.cloned.1.call-done = f32[32,256,64]{1,0,2:T(8,128)} async-done(((f32[32,256,64]{1,0,2:T(8,128)}), f32[32,256,64]{1,0,2:T(8,128)}) %all-reduce.18.cloned.1.call-update) | async-done | bytes 2097168 | tf_op jit(solution)/shard_map/psum | solution.py:58
  912.7 1.7 constant_dynamic-slice_fusion.1
  914.4 5.5 conditional.13
  914.4 1.6 copy.81
  918.4 1.5 copy.104
  919.9 2.5 broadcast_in_dim.105
  922.4 2.4 dynamic_update_slice.24
  925.5 5.8 sort.45
  931.3 17.4 %gather_fusion.1 = s32[3072]{0:T(1024)S(1)} fusion(s32[3072]{0:T(1024)S(1)} %copy-done.1, s32[3072]{0:T(1024)S(1)} %fusion.49), kind=kCustom, calls=%fused_computation.1 | custom fusion | bytes 36864 | tf_op jit(solution)/shard_map/gather | solution.py:30
  949.4 6.6 all-to-all-start.1
  956.0 2.8 copy.67
  958.8 12.2 %gather_fusion = f32[3072,64]{1,0:T(8,128)} fusion(f32[3072,64]{1,0:T(8,128)} %copy.67, s32[3072]{0:T(1024)S(1)} %fusion.49), kind=kCustom, calls=%fused_computation | custom fusion | bytes 1585152 | tf_op jit(solution)/shard_map/gather | solution.py:29
  971.1 3.1 reshape.118
  974.2 10.1 all-to-all-start
  985.9 5.8 sort.46
  991.7 9.3 all-to-all-done
  1001.5 4.5 reduce.7
  1006.1 2.7 reshape.119
  1008.7 12.2 %gather_fusion.2 = f32[3072,64]{1,0:T(8,128)} fusion(f32[3072,64]{1,0:T(8,128)} %bitcast.141, s32[3072]{0:T(1024)S(1)} %fusion.50), kind=kCustom, calls=%fused_computation.2 | custom fusion | bytes 1585152 | tf_op jit(solution)/shard_map/gather | solution.py:34
  1021.0 2.8 copy.84
  1023.8 56.9 %all-reduce.20.cloned.1.call-done = f32[64,256,64]{1,0,2:T(8,128)} async-done(((f32[64,256,64]{1,0,2:T(8,128)}), f32[64,256,64]{1,0,2:T(8,128)}) %all-reduce.20.cloned.1.call-update) | async-done | bytes 4194320 | tf_op jit(solution)/shard_map/psum | solution.py:58
  1081.8 2.1 stack.2
  1083.9 3.0 fusion.45
  1087.0 12.3 %fusion.40 = f32[12,256,64]{1,2,0:T(8,128)S(1)} fusion(f32[12,256,64]{1,2,0:T(8,128)S(1)} %copy-done.4, f32[1,12,4,256,256]{4,3,2,1,0:T(8,128)} %param.28, f32[12,4,256,64]{2,0,3,1:T(8,128)S(1)} %fusion.45), kind=kOutput, calls=%fused_computation.45 | convolution fusion | flops 2416115712 | bytes 17301504 | tf_op jit(solution)/shard_map/scwv,scwr->svr/dot_general | solution.py:68
  1099.3 4.0 fusion.37
  1103.3 2.8 copy.92
  1106.0 12.2 %gather_fusion.3 = f32[3072,64]{1,0:T(8,128)} fusion(f32[3072,64]{1,0:T(8,128)} %bitcast.142, s32[3072]{0:T(1024)S(1)} %broadcast_clamp_fusion), kind=kCustom, calls=%fused_computation.3 | custom fusion | bytes 1585152 | tf_op jit(solution)/shard_map/gather | solution.py:75
  1118.3 3.1 reshape.120
  1121.4 7.0 all-to-all-start.2
  1128.3 5.8 sort.47
  1135.6 9.0 all-to-all-done.2
  1144.6 4.5 reduce.8
  1149.1 2.6 reshape.121
  1151.7 12.2 %gather_fusion.4 = f32[3072,64]{1,0:T(8,128)} fusion(f32[3072,64]{1,0:T(8,128)} %bitcast.143, s32[3072]{0:T(1024)S(1)} %fusion.51), kind=kCustom, calls=%fused_computation.4 | custom fusion | bytes 1585152 | tf_op jit(solution)/shard_map/gather | solution.py:78
  1163.9 2.7 copy.87
  (79 shorter events, 24.0 us)
Async XLA Ops:
  7.2 1092.1 %copy-start = (f32[1,12,256,256]{3,2,1,0:T(8,128)S(1)}, f32[1,12,256,256]{3,2,1,0:T(8,128)}, u32[]{:S(2)}) copy-start(f32[1,12,256,256]{3,2,1,0:T(8,128)} %param.27) | copy-start | bytes 9437188
  7.2 147.2 %all-reduce.8.cloned.1.call-start = ((), (), s32[]{:S(2)}) async-start(), calls=%async_computation.3 | async-start | bytes 131072 | tf_op jit(solution)/shard_map/psum | solution.py:58
  8.0 289.8 %all-reduce.10.cloned.1.call-start = ((), (), s32[]{:S(2)}) async-start(), calls=%async_computation.4 | async-start | bytes 262144 | tf_op jit(solution)/shard_map/psum | solution.py:58
  156.0 0.7 copy-start.8
  156.7 288.4 %all-reduce.12.cloned.1.call-start = ((), (), s32[]{:S(2)}) async-start(), calls=%async_computation.5 | async-start | bytes 524288 | tf_op jit(solution)/shard_map/psum | solution.py:58
  301.0 0.7 copy-start.5
  301.7 295.2 %all-reduce.14.cloned.1.call-start = ((), (), s32[]{:S(2)}) async-start(), calls=%async_computation.6 | async-start | bytes 1048576 | tf_op jit(solution)/shard_map/psum | solution.py:58
  450.6 303.3 %all-reduce.16.cloned.1.call-start = ((), (), s32[]{:S(2)}) async-start(), calls=%async_computation.7 | async-start | bytes 2097152 | tf_op jit(solution)/shard_map/psum | solution.py:58
  599.9 155.7 %copy-start.2 = (f32[1,256,256]{2,1,0:T(8,128)S(1)}, f32[1,256,256]{2,1,0:T(8,128)}, u32[]{:S(2)}) copy-start(f32[1,256,256]{2,1,0:T(8,128)} %param.25) | copy-start | bytes 786436
  599.9 155.7 %copy-start.3 = (f32[1,256,64]{1,2,0:T(8,128)S(1)}, f32[1,256,64]{1,2,0:T(8,128)}, u32[]{:S(2)}) copy-start(f32[1,256,64]{1,2,0:T(8,128)} %param.24) | copy-start | bytes 196612
  603.4 309.3 %all-reduce.18.cloned.1.call-start = ((), (), s32[]{:S(2)}) async-start(), calls=%async_computation.8 | async-start | bytes 4194304 | tf_op jit(solution)/shard_map/psum | solution.py:58
  760.9 319.8 %all-reduce.20.cloned.1.call-start = ((), (), s32[]{:S(2)}) async-start(), calls=%async_computation.9 | async-start | bytes 8388608 | tf_op jit(solution)/shard_map/psum | solution.py:58
  924.8 0.7 copy-start.1
  949.4 24.8 %all-to-all-start.1 = ((s32[128,1,24]{2,1,0:T(1,128)}), s32[128,1,24]{2,1,0:T(1,128)S(1)}, u32[]{:S(2)}, u32[]{:S(2)}) async-start(s32[128,1,24]{2,1,0:T(1,128)} %bitcast.40), calls=%async_computation.1 | async-start | bytes 131072 | tf_op jit(solution)/shard_map/all_to_all | solution.py:11
  974.2 26.8 %all-to-all-start = ((f32[128,1,1536]{2,1,0:T(1,128)}), f32[128,1,1536]{2,1,0:T(1,128)}, u32[]{:S(2)}, u32[]{:S(2)}) async-start(f32[128,1,1536]{2,1,0:T(1,128)} %reshape.118), calls=%async_computation | async-start | bytes 1572864 | tf_op jit(solution)/shard_map/all_to_all | solution.py:10
  1021.0 60.8 %copy-start.6 = (f32[1,256,64]{1,0,2:T(1,128)S(1)}, f32[1,256,64]{1,0,2:T(1,128)}, u32[]{:S(2)}) copy-start(f32[1,256,64]{1,0,2:T(1,128)} %constant_dynamic-slice_fusion.2) | copy-start | bytes 196612
  1021.0 60.8 %copy-start.7 = (f32[1,256,64]{1,0,2:T(1,128)S(1)}, f32[1,256,64]{1,0,2:T(1,128)}, u32[]{:S(2)}) copy-start(f32[1,256,64]{1,0,2:T(1,128)} %constant_dynamic-slice_fusion.1) | copy-start | bytes 196612
  1021.0 60.8 %copy-start.9 = (f32[1,256,64]{1,0,2:T(1,128)S(1)}, f32[1,256,64]{1,0,2:T(1,128)}, u32[]{:S(2)}) copy-start(f32[1,256,64]{1,0,2:T(1,128)} %all-reduce.8.cloned.1.call-done) | copy-start | bytes 196612
  1021.0 63.0 %copy-start.10 = (s32[1,12,4]{1,2,0:T(4,128)S(1)}, s32[1,12,4]{1,2,0:T(4,128)}, u32[]{:S(2)}) copy-start(s32[1,12,4]{1,2,0:T(4,128)} %param.29) | copy-start | bytes 580
  1083.9 3.1 copy-start.4
  1121.4 23.3 %all-to-all-start.2 = ((f32[128,1,1536]{2,1,0:T(1,128)}), f32[128,1,1536]{2,1,0:T(1,128)}, u32[]{:S(2)}, u32[]{:S(2)}) async-start(f32[128,1,1536]{2,1,0:T(1,128)} %reshape.120), calls=%async_computation.2 | async-start | bytes 1572864 | tf_op jit(solution)/shard_map/all_to_all | solution.py:14
Sparse Core Ops, SparseCore 0:
  13.3 141.0 all-reduce.7
  160.4 137.2 all-reduce.9
  303.1 141.9 all-reduce.11
  450.7 146.1 all-reduce.13
  603.6 150.2 all-reduce.15
  761.0 151.6 all-reduce.17
  925.0 155.6 all-reduce.19
where the time goes:
time: 1170 us
  waiting for transfers between devices  954 us (82%)
  local copies, waits for them, and re-layouts  130 us (11%)
  other arithmetic  28.7 us (2%)
  starting transfers between devices  24 us (2%)
  matrix products  21.7 us (2%)
  between operations  14.5 us (1%)
    psum x7, waiting for transfers between devices, per_device(): summed = lax.psum(level_slots, ('row', 'col'))  936 us
  transfers between devices with their start and end apart: 10, of which 9 were waited for; matrix products, arithmetic and copies ran while one was open for 7% of the time, Pallas kernels for 0%

commit v1 on v0

v1 whole, which is shorter than its diff:
```python
import functools

import jax
import jax.numpy as jnp
from jax import lax
from jax.experimental import pallas as pl
from jax.experimental.pallas import tpu as pltpu
from jax.sharding import PartitionSpec as P

MESH = pl.DeviceIdType.MESH
F32 = jnp.float32
BF16 = jnp.bfloat16
I32 = jnp.int32
NN = (((1,), (0,)), ((), ()))
NT = (((1,), (1,)), ((), ()))

DEV = 128
LEVELS = 7
W = 256
R = 64
LEAF = 12
NCOUP = 4
ROWS = 3072
SEG = 24
HALF = 12
MSG = HALF + 1
PITCH = 16


def mesh_id(device):
    return (lax.shift_right_logical(device, 4), device & 15)


def split(value):
    high = value.astype(BF16)
    return high, (value - high.astype(F32)).astype(BF16)


def pieces(x):
    high, low = split(x)
    return jnp.concatenate([high, low], 0), high


def dot3(x2, xh, weights, dims):
    wh, wl = split(weights)
    n = xh.shape[0]
    both = lax.dot_general(x2, wh, dims, preferred_element_type=F32)
    cross = lax.dot_general(xh, wl, dims, preferred_element_type=F32)
    return both[:n] + both[n:] + cross


def iota(shape, axis):
    return lax.broadcasted_iota(I32, shape, axis)


def within(index, size):
    return jnp.clip(index, 0, size - 1)


def onehot(mask):
    return jnp.where(mask, 1.0, 0.0)


def trailing_zeros(number):
    total = jnp.int32(0)
    for k in range(1, 8):
        total = total + jnp.where((number & ((1 << k) - 1)) == 0, 1, 0)
    return total


def gather_pairs(steps, source, table, second, store):
    left = iota((1, 128), 1) < R

    def step(k, carry):
        for l in range(128):
            a = table[first(k), l]
            b = table[second(k), l]
            store(k, l, jnp.where(left, source[pl.ds(a, 1), :], source[pl.ds(b, 1), :]))
        return carry

    first, second = second
    lax.fori_loop(0, steps, step, 0)


def double_halves(value):
    left = iota(value.shape, value.ndim - 1) < R
    swapped = pltpu.roll(value, R, value.ndim - 1)
    return jnp.where(left, value, swapped), jnp.where(left, swapped, value)


def kernel(
    rhs_hbm, map_hbm, seprhs_hbm, sepinv_hbm, seppar_hbm, leafinv_hbm, coup_hbm, links,
    x_hbm, sep_hbm,
    rhs, rmap, seprhs, sepinv, seppar, leafinv, coup,
    doubled, sbuf, rbuf, received, grouped, solved, sbuf2, rbuf2, returned, xout,
    anc, sepout, acc, qt, cums, labels, pos_v, idx_v, idx, idx_r, idx_pos,
    in_sem, loc_sem, tree_send, tree_recv, a_send, a_recv, b_send, b_recv,
):
    me = lax.axis_index("row") * 16 + lax.axis_index("col")

    loads = [
        pltpu.make_async_copy(s, d, in_sem.at[i])
        for i, (s, d) in enumerate(
            (
                (sepinv_hbm, sepinv), (seprhs_hbm, seprhs), (map_hbm, rmap), (seppar_hbm, seppar),
                (rhs_hbm, rhs), (coup_hbm, coup), (leafinv_hbm, leafinv),
            )
        )
    ]
    for load in loads:
        load.start()

    barrier = pltpu.get_barrier_semaphore()

    def greet(k):
        pl.semaphore_signal(barrier, inc=1, device_id=mesh_id(me ^ k), device_id_type=MESH)

    for k in range(1, 8):
        greet(k)

    def greet8(i, carry):
        for k in range(8):
            greet(i * 8 + k)
        return carry

    lax.fori_loop(1, DEV // 8, greet8, 0)

    own = 6 - trailing_zeros(me + 1)
    partner_own = 6 - trailing_zeros(me + 2)
    reach = lax.shift_right_logical(jnp.int32(32), jnp.clip(own, 0, 5))
    inner = (own >= 0) & (own < 6)

    def tree_copy(m, to, which):
        return pltpu.make_async_remote_copy(
            src_ref=anc.at[m], dst_ref=anc.at[m], send_sem=tree_send.at[m, which], recv_sem=tree_recv.at[m],
            device_id=mesh_id(to), device_id_type=MESH,
        )

    def push(m, act):
        @pl.when(inner)
        def _():
            act(tree_copy(m, me - reach, 0))
            act(tree_copy(m, me + reach, 1))

        @pl.when((own == 6) & (m > partner_own))
        def _():
            act(tree_copy(m, me + 1, 0))

    def tree_wait(m):
        tree_copy(m, me, 0).wait_recv()

    def solve_own(m, target):
        t2, th = pieces(target)
        x = dot3(t2, th, sepinv[...], NT)
        anc[m] = x
        sepout[...] = x
        push(m, lambda c: c.start())

    def own_step(m):
        p2, ph = pieces(anc[m - 1])
        solve_own(m, seprhs[...] - dot3(p2, ph, seppar[...], NN))

    loads[0].wait()
    loads[1].wait()
    loads[3].wait()
    pl.semaphore_wait(barrier, DEV - 1)

    @pl.when(own == 0)
    def _():
        solve_own(0, seprhs[...])

    @pl.when(own == 1)
    def _():
        tree_wait(0)
        push(0, lambda c: c.start())
        own_step(1)

    @pl.when(own < 0)
    def _():
        sepout[...] = jnp.zeros_like(sepout)

    loads[2].wait()
    rows = rmap[...]
    dest = lax.shift_right_logical(lax.shift_right_logical(rows, 10) * 171, 9)
    local = rows - dest * ROWS
    for j in range(12):
        for h in range(2):
            r = 2 * j + h
            qt[j * 128:(j + 1) * 128, h * 128:(h + 1) * 128] = onehot(
                iota((128, 128), 0) == dest[r:r + 1, :]
            ).astype(BF16)
    tri = onehot((iota((256, 384), 0) < iota((256, 384), 1)) | (iota((256, 384), 1) >= 256)).astype(BF16)
    cums[...] = lax.dot_general(qt[...], tri, NN, preferred_element_type=F32)
    carry = jnp.zeros((128, 128), F32)
    table = jnp.zeros((128, 128), F32)
    sub32 = iota((32, 128), 0)
    lane = iota((1, 128), 1)
    for j in range(12):
        parts = []
        for h in range(2):
            r = 2 * j + h
            q = qt[j * 128:(j + 1) * 128, h * 128:(h + 1) * 128].astype(F32)
            rank = jnp.sum(q * (cums[j * 128:(j + 1) * 128, h * 128:(h + 1) * 128] + carry), axis=0, keepdims=True)
            rank = rank.astype(I32)
            hit = sub32 == rank
            loc = local[r:r + 1, :]
            parts.append(
                jnp.concatenate(
                    [
                        jnp.where(hit, float(r), 0.0),
                        jnp.where(hit, lane.astype(F32), 0.0),
                        jnp.where(hit, lax.shift_right_logical(loc, 7).astype(F32), 0.0),
                        jnp.where(hit, (loc & 127).astype(F32), 0.0),
                    ],
                    0,
                )
            )
            at = dest[r:r + 1, :] * PITCH + rank + jnp.where(rank >= HALF, DEV * PITCH - HALF, 0)
            pos_v[r:r + 1, :] = within(at, 2 * DEV * PITCH)
        digits = jnp.concatenate(parts, 1).astype(BF16)
        table = table + lax.dot_general(digits, qt[j * 128:(j + 1) * 128, :], NT, preferred_element_type=F32)
        carry = carry + cums[j * 128:(j + 1) * 128, 256:384]
    idx_v[0:24, :] = within((table[0:24] * 128.0 + table[32:56]).astype(I32), ROWS)
    to_idx = pltpu.make_async_copy(idx_v.at[pl.ds(0, 24)], idx, loc_sem.at[0])
    to_idx.start()
    to_pos = pltpu.make_async_copy(pos_v, idx_pos, loc_sem.at[1])
    to_pos.start()
    lab = table[64:96] * 128.0 + table[96:128]
    labels[...] = jnp.concatenate([lab, jnp.zeros((96, 128), F32)], 0).T

    loads[4].wait()

    def double_rhs(j, carry):
        block = rhs[:, pl.ds(pl.multiple_of(j * 128, 128), 128)]
        doubled[pl.ds(pl.multiple_of(j * 128, 128), 128), :] = jnp.concatenate([block, block], 0).T
        return carry

    lax.fori_loop(0, ROWS // 128, double_rhs, 0, unroll=4)

    to_idx.wait()
    to_pos.wait()

    def put_send(k, l, row):
        sbuf[l, pl.ds(k, 1), :] = row

    gather_pairs(HALF, doubled, idx, (lambda k: k, lambda k: k + HALF), put_send)
    for l in range(128):
        sbuf[l, HALF:MSG, :] = labels[l:l + 1, :]

    def exchange(src, dst, send, recv):
        def go(k, carry):
            to = me ^ k
            pltpu.make_async_remote_copy(
                src_ref=src.at[to], dst_ref=dst.at[me], send_sem=send, recv_sem=recv,
                device_id=mesh_id(to), device_id_type=MESH,
            ).start()
            return carry

        lax.fori_loop(1, DEV, go, 0)
        mine = pltpu.make_async_copy(src.at[me], dst.at[me], loc_sem.at[2])
        mine.start()
        mine.wait()

    def exchange_wait(src, dst, sem):
        n = DEV - 1
        pltpu.make_async_copy(src.at[pl.ds(0, n)], dst.at[pl.ds(0, n)], sem).wait()

    exchange(sbuf, rbuf, a_send, a_recv)

    loads[5].wait()
    acc[...] = jnp.zeros_like(acc)

    def level(m, carry):
        @pl.when((m != own) & ((own < 0) | (own > 1) | (m > own)))
        def _():
            tree_wait(m)

        @pl.when((m < own) & (own > 1) | (m > own) & False)
        def _():
            push(m, lambda c: c.start())

        @pl.when((m == own) & (own > 1))
        def _():
            own_step(m)

        p = LEVELS - 1 - m
        x2, xh = pieces(anc[m])

        def blocks(g, c0):
            for u in range(4):
                s = g * 4 + u
                which = jnp.int32(0)
                found = jnp.int32(0)
                for c in range(NCOUP):
                    here = jnp.where(links[s, c] == p, 1, 0)
                    which = jnp.where(here > 0, c, which)
                    found = found + here
                term = dot3(x2, xh, coup[s * NCOUP + which], NN)
                acc[s] += jnp.where(found > 0, term, 0.0)
            return c0

        lax.fori_loop(0, LEAF // 4, blocks, 0)
        return carry

    lax.fori_loop(0, LEVELS, level, 0)

    exchange_wait(sbuf, rbuf, a_recv)
    for p in range(128):
        labels[p:p + 1, :] = rbuf[p, HALF:MSG, :]
    got = labels[...].T[0:32].astype(I32)
    high = lax.shift_right_logical(got, 7)
    low = got & 127
    inverse = jnp.zeros((64, 128), F32)
    for j in range(12):
        aa, bb = [], []
        for h in range(2):
            r = 2 * j + h
            at = lane * PITCH + (r % HALF + (r // HALF) * DEV * PITCH)
            hit = sub32 == high[r:r + 1, :]
            aa.append(
                jnp.concatenate(
                    [
                        jnp.where(hit, lax.shift_right_logical(at, 6).astype(F32), 0.0),
                        jnp.where(hit, (at & 63).astype(F32), 0.0),
                    ],
                    0,
                )
            )
            bb.append(onehot(iota((128, 128), 0) == low[r:r + 1, :]))
        inverse = inverse + lax.dot_general(
            jnp.concatenate(aa, 1).astype(BF16), jnp.concatenate(bb, 1).astype(BF16), NT, preferred_element_type=F32
        )
    idx_v[0:24, :] = within((inverse[0:24] * 64.0 + inverse[32:56]).astype(I32), 2 * DEV * PITCH)
    idx_v[24:48, :] = within(((high & 1) * (ROWS // 2) + lax.shift_right_logical(high, 1) * 128 + low)[0:24], ROWS)
    to_idx = pltpu.make_async_copy(idx_v, idx_r, loc_sem.at[0])
    to_idx.start()

    def double_message(src, dst, n, p):
        lo2, hi2 = double_halves(src[p])
        dst[pl.ds(pl.multiple_of(p * PITCH, PITCH), n), :] = lo2
        dst[pl.ds(pl.multiple_of((p + DEV) * PITCH, PITCH), n), :] = hi2

    def double_received(p, carry):
        double_message(rbuf, received, MSG, p)
        return carry

    lax.fori_loop(0, DEV, double_received, 0, unroll=8)
    to_idx.wait()

    def put_grouped(k, l, row):
        grouped[pl.ds(k * 128 + l, 1), :] = row

    gather_pairs(LEAF, received, idx_r, (lambda k: 2 * k, lambda k: 2 * k + 1), put_grouped)

    loads[6].wait()

    def leaf(g, carry):
        for u in range(4):
            t = g * 4 + u
            at = pl.multiple_of(t * 128, 128)
            both = grouped[pl.ds(at, 128), :].T
            target = jnp.concatenate([both[:R], both[R:]], 1) - acc[t]
            t2, th = pieces(target)
            x = dot3(t2, th, leafinv[t], NT)
            solved[pl.ds(at, 128), :] = jnp.concatenate([x[:, :128], x[:, :128]], 0).T
            solved[pl.ds(pl.multiple_of(at + ROWS // 2, 128), 128), :] = jnp.concatenate([x[:, 128:], x[:, 128:]], 0).T
        return carry

    lax.fori_loop(0, LEAF // 4, leaf, 0)

    def put_back(k, l, row):
        sbuf2[l, pl.ds(k, 1), :] = row

    gather_pairs(HALF, solved, idx_r, (lambda k: k + 24, lambda k: k + 24 + HALF), put_back)
    exchange(sbuf2, rbuf2, b_send, b_recv)
    out_sep = pltpu.make_async_copy(sepout, sep_hbm, loc_sem.at[3])
    out_sep.start()

    exchange_wait(sbuf, rbuf, a_send)

    def settle(m, carry):
        @pl.when(m <= own)
        def _():
            push(m, lambda c: c.wait_send())

        return carry

    lax.fori_loop(0, LEVELS, settle, 0)
    out_sep.wait()

    exchange_wait(sbuf2, rbuf2, b_recv)

    def double_returned(p, carry):
        double_message(rbuf2, returned, HALF, p)
        return carry

    lax.fori_loop(0, DEV, double_returned, 0, unroll=8)

    left = iota((1, 128), 1) < R

    def restore(j, carry):
        for l in range(128):
            a = idx_pos[2 * j, l]
            b = idx_pos[2 * j + 1, l]
            grouped[pl.ds(j * 128 + l, 1), :] = jnp.where(left, returned[pl.ds(a, 1), :], returned[pl.ds(b, 1), :])
        both = grouped[pl.ds(pl.multiple_of(j * 128, 128), 128), :].T
        xout[:, pl.ds(pl.multiple_of(j * 256, 256), 256)] = jnp.concatenate([both[:R], both[R:]], 1)
        return carry

    lax.fori_loop(0, LEAF, restore, 0)
    exchange_wait(sbuf2, rbuf2, b_send)
    out_x = pltpu.make_async_copy(xout, x_hbm, loc_sem.at[0])
    out_x.start()
    out_x.wait()


def per_device(rhs_held, row_map, sep_rhs, sep_inverse, sep_parent, leaf_inverse, leaf_coupling, leaf_links):
    hbm = pl.BlockSpec(memory_space=pltpu.HBM)
    vmem = pltpu.VMEM
    x, sep = pl.pallas_call(
        kernel,
        out_shape=(jax.ShapeDtypeStruct((R, ROWS), F32), jax.ShapeDtypeStruct((R, W), F32)),
        in_specs=[hbm] * 7 + [pl.BlockSpec(memory_space=pltpu.SMEM)],
        out_specs=(hbm, hbm),
        scratch_shapes=[
            vmem((R, ROWS), F32),
            vmem((24, 128), I32),
            vmem((R, W), F32),
            vmem((W, W), F32),
            vmem((W, W), F32),
            vmem((LEAF, W, W), F32),
            vmem((LEAF * NCOUP, W, W), F32),
            vmem((ROWS, 128), F32),
            vmem((DEV, MSG, 128), F32),
            vmem((DEV, MSG, 128), F32),
            vmem((2 * DEV * PITCH, 128), F32),
            vmem((ROWS // 2, 128), F32),
            vmem((ROWS, 128), F32),
            vmem((DEV, HALF, 128), F32),
            vmem((DEV, HALF, 128), F32),
            vmem((2 * DEV * PITCH, 128), F32),
            vmem((R, ROWS), F32),
            vmem((LEVELS, R, W), F32),
            vmem((R, W), F32),
            vmem((LEAF, R, W), F32),
            vmem((12 * 128, 256), BF16),
            vmem((12 * 128, 384), F32),
            vmem((128, 128), F32),
            vmem((24, 128), I32),
            vmem((48, 128), I32),
            pltpu.SMEM((24, 128), I32),
            pltpu.SMEM((48, 128), I32),
            pltpu.SMEM((24, 128), I32),
            pltpu.SemaphoreType.DMA((7,)),
            pltpu.SemaphoreType.DMA((4,)),
            pltpu.SemaphoreType.DMA((LEVELS, 2)),
            pltpu.SemaphoreType.DMA((LEVELS,)),
            pltpu.SemaphoreType.DMA,
            pltpu.SemaphoreType.DMA,
            pltpu.SemaphoreType.DMA,
            pltpu.SemaphoreType.DMA,
        ],
        compiler_params=pltpu.CompilerParams(
            collective_id=0, has_side_effects=True, vmem_limit_bytes=56 << 20
        ),
        name="gmrf_solve",
    )(
        rhs_held.T,
        row_map.reshape(24, 128),
        sep_rhs[0].T,
        sep_inverse[0],
        sep_parent[0],
        leaf_inverse[0],
        leaf_coupling[0].reshape(LEAF * NCOUP, W, W),
        leaf_links[0],
    )
    return x.T, sep.T[None]


def solution(mesh):
    in_specs = (
        P(("row", "col"), None),
        P(("row", "col")),
        P(("row", "col"), None, None),
        P(("row", "col"), None, None),
        P(("row", "col"), None, None),
        P(("row", "col"), None, None, None),
        P(("row", "col"), None, None, None, None),
        P(("row", "col"), None, None),
    )
    out_specs = (P(("row", "col"), None), P(("row", "col"), None, None))
    return jax.shard_map(per_device, mesh=mesh, in_specs=in_specs, out_specs=out_specs, check_vma=False)
```

time: 1170 us -> 88.1 us (0.08)
  waiting for transfers between devices: 954 us -> 0 us
  local copies, waits for them, and re-layouts: 130 us -> 4.9 us
  Pallas kernels: 0 us -> 82.3 us
  other arithmetic: 28.7 us -> 0 us
  starting transfers between devices: 24 us -> 0 us
  matrix products: 21.7 us -> 0 us
  between operations: 14.5 us -> 0.64 us
    psum x7 -> x0, waiting for transfers between devices: 936 us -> none  [per_device(): summed = lax.psum(level_slots, ('row', 'col'))]
    pallas_call x0 -> x1, Pallas kernels: none -> 82.3 us  [per_device(): pl.pallas_call(kernel, out_shape=(jax.ShapeDtypeStruct((R, ROWS), F32), j...]
    gather x5 -> x0, local copies, waits for them, and re-layouts: 66.3 us -> none  [the longest x1 17.4 us: per_device(): send_tags = row_map[by_label].reshape(devices, segment)]
    all_to_all x3 -> x0, starting transfers between devices: 23.7 us -> none  [the longest x2 17.1 us: regroup_rows(): lax.all_to_all(payload, ('row', 'col'), split_axis=0, concat_axis=0, tile...]
    dot_general x5 -> x0, matrix products: 21.7 us -> none  [the longest x1 12.3 us: per_device(): jnp.einsum('scwv,scwr->svr', leaf_coupling[0], picked, precision=lax.Prec...]
    all_to_all x3 -> x0, waiting for transfers between devices: 18.3 us -> none  [the longest x2 18.3 us: regroup_rows(): lax.all_to_all(payload, ('row', 'col'), split_axis=0, concat_axis=0, tile...]
    sort x3 -> x0, other arithmetic: 17.3 us -> none  [the longest x1 5.76 us: per_device(): placement = jnp.argsort(local_rows)]
    unnamed x28 -> x2, local copies, waits for them, and re-layouts: 19.1 us -> 3.54 us
  transfers between devices with their start and end apart: 10 -> 0, of which waited for: 9 -> 0; matrix products, arithmetic and copies ran while one was open for 7% -> 0% of each run, Pallas kernels for 0% -> 0%
where the time goes in v1:
time: 88.1 us; the launch traced here: 87.9 us
  Pallas kernels  82.3 us (93%)
  local copies, waits for them, and re-layouts  4.9 us (6%)
    pallas_call x1, Pallas kernels, per_device(): pl.pallas_call(kernel, out_shape=(jax.ShapeDtypeStruct((R, ROWS), F32), j...  82.3 us
    unnamed x2, local copies, waits for them, and re-layouts  3.54 us

profile of v1, /device:TPU:1, one launch (start us, length us, event | category | flops | bytes accessed | tf_op | source)
XLA Modules:
  0.0 87.9 jit_solution(5911587562709327871)
XLA Ops:
  0.6 1.4 %copy.10.links = s32[12,4]{1,0:T(8,128)} copy(s32[12,4]{0,1:T(4,128)} %bitcast.23) | data formatting | bytes 384 | tf_op jit(solution)/shard_map/squeeze | solution.py:475
  2.0 82.3 %gmrf_solve.1 = (f32[64,3072]{1,0:T(8,128)}, f32[64,256]{1,0:T(8,128)}) custom-call(f32[64,3072]{1,0:T(8,128)} %bitcast.16, s32[24,128]{1,0:T(8,128)} %bitcast.22, f32[64,256]{1,0:T(8,128)} %bitcast.20, f32[256,256]{1,0:T(8,128)} %bitcast.18, f32[256,256]{1,0:T(8,128)} %bitcast.19, f32[12,256,256]{2,1,0:T(8,128)} %bitcast.15, f32[48,256,256]{2,1,0:T(8,128)} %bitcast.14, ...), custom_call_target="tpu_custom_call" | custom-call | tf_op jit(solution)/shard_map/gmrf_solve/pallas_call | solution.py:420
  84.3 2.1 %copy.13 = f32[3072,64]{0,1:T(8,128)} copy(f32[3072,64]{0,1:T(8,128)} %bitcast.17) | data formatting | bytes 1572864
  86.4 1.5 %copy.14 = f32[1,256,64]{1,2,0:T(8,128)} copy(f32[1,256,64]{1,2,0:T(8,128)} %bitcast.21) | data formatting | bytes 131072

commit v2 on v1

--- a/solution.py
+++ b/solution.py
@@ -24,6 +24,8 @@
 SEG = 24
 HALF = 12
 MSG = HALF + 1
+SPREAD = 37
+EARLY = (1, 1, 24, 64, 100)
 PITCH = 16
 
 
@@ -88,13 +90,26 @@
     return jnp.where(left, value, swapped), jnp.where(left, swapped, value)
 
 
+def double_messages(src, dst, n):
+    def group(g, carry):
+        lo2, hi2 = double_halves(src[pl.ds(g * 8, 8)])
+        for i in range(8):
+            at = pl.multiple_of((g * 8 + i) * PITCH, PITCH)
+            dst[pl.ds(at, n), :] = lo2[i]
+            dst[pl.ds(pl.multiple_of(at + DEV * PITCH, PITCH), n), :] = hi2[i]
+        return carry
+
+    lax.fori_loop(0, DEV // 8, group, 0)
+
+
 def kernel(
     rhs_hbm, map_hbm, seprhs_hbm, sepinv_hbm, seppar_hbm, leafinv_hbm, coup_hbm, links,
-    x_hbm, sep_hbm,
+    came_hbm, pos_hbm, sep_hbm,
     rhs, rmap, seprhs, sepinv, seppar, leafinv, coup,
-    doubled, sbuf, rbuf, received, grouped, solved, sbuf2, rbuf2, returned, xout,
-    anc, sepout, acc, qt, cums, labels, pos_v, idx_v, idx, idx_r, idx_pos,
-    in_sem, loc_sem, tree_send, tree_recv, a_send, a_recv, b_send, b_recv,
+    doubled, sbuf, rbuf, received, grouped, solved, sbuf2,
+    anc, crit, sepout, acc, qt, cums, labels, pos_v, idx_v, idx, idx_r,
+    in_sem, loc_sem, crit_send, crit_recv, part_recv, zero_send, zero_recv, five_send, five_recv,
+    scat_send, scat_recv, ag_send, ag_recv, a_send, a_recv, b_send, b_recv,
 ):
     me = lax.axis_index("row") * 16 + lax.axis_index("col")
 
@@ -126,54 +141,55 @@
     lax.fori_loop(1, DEV // 8, greet8, 0)
 
     own = 6 - trailing_zeros(me + 1)
-    partner_own = 6 - trailing_zeros(me + 2)
     reach = lax.shift_right_logical(jnp.int32(32), jnp.clip(own, 0, 5))
     inner = (own >= 0) & (own < 6)
-
-    def tree_copy(m, to, which):
+    x_at = me & 3
+    even = (me & 1) == 0
+
+    def remote(src, dst, send, recv, to):
         return pltpu.make_async_remote_copy(
-            src_ref=anc.at[m], dst_ref=anc.at[m], send_sem=tree_send.at[m, which], recv_sem=tree_recv.at[m],
-            device_id=mesh_id(to), device_id_type=MESH,
+            src_ref=src, dst_ref=dst, send_sem=send, recv_sem=recv, device_id=mesh_id(to), device_id_type=MESH
         )
 
-    def push(m, act):
+    def rows_of(first, count):
+        return anc.at[pl.ds(pl.multiple_of(first, 8), count)]
+
+    def drain(count, sem):
+        pltpu.make_async_copy(anc.at[pl.ds(0, count)], anc.at[pl.ds(0, count)], sem).wait()
+
+    def set_level(m, value):
+        anc[m * R:(m + 1) * R, :] = value
+
+    def to_children(act):
         @pl.when(inner)
         def _():
-            act(tree_copy(m, me - reach, 0))
-            act(tree_copy(m, me + reach, 1))
-
-        @pl.when((own == 6) & (m > partner_own))
-        def _():
-            act(tree_copy(m, me + 1, 0))
-
-    def tree_wait(m):
-        tree_copy(m, me, 0).wait_recv()
-
-    def solve_own(m, target):
+            act(remote(sepout, crit, crit_send.at[0], crit_recv, me - reach))
+            act(remote(sepout, crit, crit_send.at[1], crit_recv, me + reach))
+
+    def to_partner():
+        return remote(sepout, rows_of(6 * R, R), crit_send.at[0], part_recv, me + 1)
+
+    def zero_to(to, which):
+        return remote(crit, rows_of(0, R), zero_send.at[which], zero_recv, to)
+
+    def five_to():
+        return remote(sepout, rows_of(5 * R, R), five_send, five_recv, me + 2)
+
+    def finish_solve(target):
         t2, th = pieces(target)
-        x = dot3(t2, th, sepinv[...], NT)
-        anc[m] = x
-        sepout[...] = x
-        push(m, lambda c: c.start())
-
-    def own_step(m):
-        p2, ph = pieces(anc[m - 1])
-        solve_own(m, seprhs[...] - dot3(p2, ph, seppar[...], NN))
+        sepout[...] = dot3(t2, th, sepinv[...], NT)
+
+    def take_and_solve():
+        pltpu.make_async_copy(sepout, crit, crit_recv).wait()
+        p2, ph = pieces(crit[...])
+        finish_solve(seprhs[...] - dot3(p2, ph, seppar[...], NN))
 
     loads[0].wait()
     loads[1].wait()
-    loads[3].wait()
-    pl.semaphore_wait(barrier, DEV - 1)
 
     @pl.when(own == 0)
     def _():
-        solve_own(0, seprhs[...])
-
-    @pl.when(own == 1)
-    def _():
-        tree_wait(0)
-        push(0, lambda c: c.start())
-        own_step(1)
+        finish_solve(seprhs[...])
 
     @pl.when(own < 0)
     def _():
@@ -223,7 +239,7 @@
     idx_v[0:24, :] = within((table[0:24] * 128.0 + table[32:56]).astype(I32), ROWS)
     to_idx = pltpu.make_async_copy(idx_v.at[pl.ds(0, 24)], idx, loc_sem.at[0])
     to_idx.start()
-    to_pos = pltpu.make_async_copy(pos_v, idx_pos, loc_sem.at[1])
+    to_pos = pltpu.make_async_copy(pos_v, pos_hbm, loc_sem.at[1])
     to_pos.start()
     lab = table[64:96] * 128.0 + table[96:128]
     labels[...] = jnp.concatenate([lab, jnp.zeros((96, 128), F32)], 0).T
@@ -238,7 +254,6 @@
     lax.fori_loop(0, ROWS // 128, double_rhs, 0, unroll=4)
 
     to_idx.wait()
-    to_pos.wait()
 
     def put_send(k, l, row):
         sbuf[l, pl.ds(k, 1), :] = row
@@ -247,44 +262,111 @@
     for l in range(128):
         sbuf[l, HALF:MSG, :] = labels[l:l + 1, :]
 
-    def exchange(src, dst, send, recv):
+    def exchange(src, dst, send, recv, first, last):
         def go(k, carry):
-            to = me ^ k
-            pltpu.make_async_remote_copy(
-                src_ref=src.at[to], dst_ref=dst.at[me], send_sem=send, recv_sem=recv,
-                device_id=mesh_id(to), device_id_type=MESH,
-            ).start()
+            to = me ^ ((k * SPREAD) & (DEV - 1))
+            remote(src.at[to], dst.at[me], send, recv, to).start()
             return carry
 
-        lax.fori_loop(1, DEV, go, 0)
-        mine = pltpu.make_async_copy(src.at[me], dst.at[me], loc_sem.at[2])
-        mine.start()
-        mine.wait()
+        lax.fori_loop(first, last, go, 0)
 
     def exchange_wait(src, dst, sem):
         n = DEV - 1
         pltpu.make_async_copy(src.at[pl.ds(0, n)], dst.at[pl.ds(0, n)], sem).wait()
 
-    exchange(sbuf, rbuf, a_send, a_recv)
+    keep = pltpu.make_async_copy(sbuf.at[me], rbuf.at[me], loc_sem.at[2])
+    keep.start()
+    loads[3].wait()
+    pl.semaphore_wait(barrier, DEV - 1)
+
+    @pl.when(own == 0)
+    def _():
+        to_children(lambda c: c.start())
+
+    @pl.when(own == 1)
+    def _():
+        take_and_solve()
+        to_children(lambda c: c.start())
+        zero_to(me - reach, 0).start()
+        zero_to(me + reach, 1).start()
+
+    early = jnp.int32(DEV)
+    for l, count in enumerate(EARLY):
+        early = jnp.where(own == l, count, early)
+    exchange(sbuf, rbuf, a_send, a_recv, 1, early)
+
+    @pl.when((own >= 2) & (own <= 4))
+    def _():
+        take_and_solve()
+        to_children(lambda c: c.start())
+
+    @pl.when(own == 2)
+    def _():
+        set_level(1, crit[...])
+        set_level(2, sepout[...])
+        drain(R, zero_recv)
+
+        def tile(i, carry):
+            to = (me & 96) | (i // 3 * 4 + i % 3)
+            remote(rows_of(i * 8, 8), rows_of(i * 8, 8), scat_send, scat_recv.at[0], to).start()
+            return carry
+
+        lax.fori_loop(0, 24, tile, 0)
+
+    @pl.when(own == 3)
+    def _():
+        set_level(3, sepout[...])
+        for i in range(8):
+            part = rows_of(3 * R + 8 * i, 8)
+            remote(part, part, scat_send, scat_recv.at[1], (me & 112) | (i // 2 * 4 + i % 2 * 2)).start()
+
+    @pl.when(own == 4)
+    def _():
+        set_level(4, sepout[...])
+        for i in range(4):
+            part = rows_of(4 * R + 16 * i, 16)
+            remote(part, part, scat_send, scat_recv.at[2], (me & 120) | (i // 2 * 4 + i % 2 * 2)).start()
+
+    exchange(sbuf, rbuf, a_send, a_recv, early, DEV)
+
+    @pl.when(x_at != 3)
+    def _():
+        drain(8, scat_recv.at[0])
+        part = rows_of((lax.shift_right_logical(me, 2) & 7) * 24 + x_at * 8, 8)
+
+        def hand(k, carry):
+            to = me ^ k
+
+            @pl.when((to & 31) != 15)
+            def _():
+                remote(part, part, ag_send.at[0], ag_recv.at[0], to).start()
+
+            return carry
+
+        lax.fori_loop(1, 32, hand, 0)
+
+    @pl.when(even)
+    def _():
+        drain(8, scat_recv.at[1])
+        part = rows_of(3 * R + (lax.shift_right_logical(me, 2) & 3) * 16 + x_at * 4, 8)
+
+        def hand(k, carry):
+            to = me ^ k
+
+            @pl.when((to & 15) != 7)
+            def _():
+                remote(part, part, ag_send.at[1], ag_recv.at[1], to).start()
+
+            return carry
+
+        lax.fori_loop(1, 16, hand, 0)
 
     loads[5].wait()
     acc[...] = jnp.zeros_like(acc)
 
     def level(m, carry):
-        @pl.when((m != own) & ((own < 0) | (own > 1) | (m > own)))
-        def _():
-            tree_wait(m)
-
-        @pl.when((m < own) & (own > 1) | (m > own) & False)
-        def _():
-            push(m, lambda c: c.start())
-
-        @pl.when((m == own) & (own > 1))
-        def _():
-            own_step(m)
-
         p = LEVELS - 1 - m
-        x2, xh = pieces(anc[m])
+        x2, xh = pieces(anc[pl.ds(pl.multiple_of(m * R, R), R), :])
 
         def blocks(g, c0):
             for u in range(4):
@@ -292,7 +374,7 @@
                 which = jnp.int32(0)
                 found = jnp.int32(0)
                 for c in range(NCOUP):
-                    here = jnp.where(links[s, c] == p, 1, 0)
+                    here = jnp.where(links[c, s] == p, 1, 0)
                     which = jnp.where(here > 0, c, which)
                     found = found + here
                 term = dot3(x2, xh, coup[s * NCOUP + which], NN)
@@ -302,9 +384,35 @@
         lax.fori_loop(0, LEAF // 4, blocks, 0)
         return carry
 
-    lax.fori_loop(0, LEVELS, level, 0)
+    @pl.when((x_at != 3))
+    def _():
+        drain(184, ag_recv.at[0])
+
+    @pl.when((x_at == 3) & (own != 2))
+    def _():
+        drain(192, ag_recv.at[0])
+
+    lax.fori_loop(0, 3, level, 0)
+
+    @pl.when(own == 5)
+    def _():
+        take_and_solve()
+        to_children(lambda c: c.start())
+        five_to().start()
+        set_level(4, crit[...])
+        set_level(5, sepout[...])
+
+    @pl.when(even)
+    def _():
+        drain(16, scat_recv.at[2])
+        part = rows_of(4 * R + (lax.shift_right_logical(me, 2) & 1) * 32 + x_at * 8, 16)
+        for low in (0, 2, 4, 6, 7):
+            @pl.when((me & 7) != low)
+            def _():
+                remote(part, part, ag_send.at[2], ag_recv.at[2], (me & 120) | low).start()
 
     exchange_wait(sbuf, rbuf, a_recv)
+    keep.wait()
     for p in range(128):
         labels[p:p + 1, :] = rbuf[p, HALF:MSG, :]
     got = labels[...].T[0:32].astype(I32)
@@ -335,22 +443,47 @@
     to_idx = pltpu.make_async_copy(idx_v, idx_r, loc_sem.at[0])
     to_idx.start()
 
-    def double_message(src, dst, n, p):
-        lo2, hi2 = double_halves(src[p])
-        dst[pl.ds(pl.multiple_of(p * PITCH, PITCH), n), :] = lo2
-        dst[pl.ds(pl.multiple_of((p + DEV) * PITCH, PITCH), n), :] = hi2
-
-    def double_received(p, carry):
-        double_message(rbuf, received, MSG, p)
-        return carry
-
-    lax.fori_loop(0, DEV, double_received, 0, unroll=8)
+    double_messages(rbuf, received, MSG)
     to_idx.wait()
 
     def put_grouped(k, l, row):
         grouped[pl.ds(k * 128 + l, 1), :] = row
 
     gather_pairs(LEAF, received, idx_r, (lambda k: 2 * k, lambda k: 2 * k + 1), put_grouped)
+
+    @pl.when(own == 6)
+    def _():
+        take_and_solve()
+        to_partner().start()
+        set_level(5, crit[...])
+        set_level(6, sepout[...])
+
+    @pl.when(even)
+    def _():
+        drain(56, ag_recv.at[1])
+        drain(48, ag_recv.at[2])
+
+    @pl.when(~even & ((me & 15) != 7))
+    def _():
+        drain(64, ag_recv.at[1])
+
+    @pl.when((me & 7) == 7)
+    def _():
+        drain(64, ag_recv.at[2])
+
+    lax.fori_loop(3, 5, level, 0)
+
+    @pl.when(x_at == 3)
+    def _():
+        drain(R, five_recv)
+
+    lax.fori_loop(5, 6, level, 0)
+
+    @pl.when(~even)
+    def _():
+        drain(R, part_recv)
+
+    lax.fori_loop(6, 7, level, 0)
 
     loads[6].wait()
 
@@ -372,56 +505,95 @@
         sbuf2[l, pl.ds(k, 1), :] = row
 
     gather_pairs(HALF, solved, idx_r, (lambda k: k + 24, lambda k: k + 24 + HALF), put_back)
-    exchange(sbuf2, rbuf2, b_send, b_recv)
+    mine = pltpu.make_async_copy(sbuf2.at[me], came_hbm.at[me], loc_sem.at[2])
+    mine.start()
+    exchange(sbuf2, came_hbm, b_send, b_recv, 1, DEV)
     out_sep = pltpu.make_async_copy(sepout, sep_hbm, loc_sem.at[3])
     out_sep.start()
 
     exchange_wait(sbuf, rbuf, a_send)
-
-    def settle(m, carry):
-        @pl.when(m <= own)
-        def _():
-            push(m, lambda c: c.wait_send())
-
-        return carry
-
-    lax.fori_loop(0, LEVELS, settle, 0)
+    to_children(lambda c: c.wait_send())
+
+    @pl.when(own == 6)
+    def _():
+        to_partner().wait_send()
+
+    @pl.when(own == 5)
+    def _():
+        five_to().wait_send()
+
+    @pl.when(own == 1)
+    def _():
+        zero_to(me - reach, 0).wait_send()
+        zero_to(me + reach, 1).wait_send()
+
+    @pl.when(own == 2)
+    def _():
+        drain(192, scat_send)
+
+    @pl.when((own == 3) | (own == 4))
+    def _():
+        drain(64, scat_send)
+
+    @pl.when(x_at != 3)
+    def _():
+        drain(240, ag_send.at[0])
+
+    @pl.when(even)
+    def _():
+        drain(112, ag_send.at[1])
+        drain(64, ag_send.at[2])
+
+    to_pos.wait()
     out_sep.wait()
-
-    exchange_wait(sbuf2, rbuf2, b_recv)
-
-    def double_returned(p, carry):
-        double_message(rbuf2, returned, HALF, p)
-        return carry
-
-    lax.fori_loop(0, DEV, double_returned, 0, unroll=8)
-
+    mine.wait()
+    exchange_wait(sbuf2, came_hbm, b_recv)
+    exchange_wait(sbuf2, came_hbm, b_send)
+
+
+def restore_kernel(came_hbm, pos, sep_hbm, x_hbm, sepx_hbm, came, returned, grouped, xout, sem, out_sem):
+    load = pltpu.make_async_copy(came_hbm, came, sem.at[0])
+    load.start()
+    move = pltpu.make_async_copy(sep_hbm, sepx_hbm, sem.at[1])
+    move.start()
+    load.wait()
+    double_messages(came, returned, HALF)
     left = iota((1, 128), 1) < R
+
+    def put(j):
+        return pltpu.make_async_copy(
+            xout.at[:, pl.ds(pl.multiple_of(j * 256, 256), 256)],
+            x_hbm.at[:, pl.ds(pl.multiple_of(j * 256, 256), 256)],
+            out_sem,
+        )
 
     def restore(j, carry):
         for l in range(128):
-            a = idx_pos[2 * j, l]
-            b = idx_pos[2 * j + 1, l]
+            a = pos[2 * j, l]
+            b = pos[2 * j + 1, l]
             grouped[pl.ds(j * 128 + l, 1), :] = jnp.where(left, returned[pl.ds(a, 1), :], returned[pl.ds(b, 1), :])
         both = grouped[pl.ds(pl.multiple_of(j * 128, 128), 128), :].T
         xout[:, pl.ds(pl.multiple_of(j * 256, 256), 256)] = jnp.concatenate([both[:R], both[R:]], 1)
+        put(j).start()
         return carry
 
     lax.fori_loop(0, LEAF, restore, 0)
-    exchange_wait(sbuf2, rbuf2, b_send)
-    out_x = pltpu.make_async_copy(xout, x_hbm, loc_sem.at[0])
-    out_x.start()
-    out_x.wait()
+    pltpu.make_async_copy(xout, x_hbm, out_sem).wait()
+    move.wait()
 
 
 def per_device(rhs_held, row_map, sep_rhs, sep_inverse, sep_parent, leaf_inverse, leaf_coupling, leaf_links):
     hbm = pl.BlockSpec(memory_space=pltpu.HBM)
     vmem = pltpu.VMEM
-    x, sep = pl.pallas_call(
+    came, pos, sep = pl.pallas_call(
         kernel,
-        out_shape=(jax.ShapeDtypeStruct((R, ROWS), F32), jax.ShapeDtypeStruct((R, W), F32)),
+        out_shape=(
+            jax.ShapeDtypeStruct((DEV, HALF, 128), F32),
+            jax.ShapeDtypeStruct((24, 128), I32),
+            jax.ShapeDtypeStruct((R, W), F32),
+        ),
         in_specs=[hbm] * 7 + [pl.BlockSpec(memory_space=pltpu.SMEM)],
-        out_specs=(hbm, hbm),
+        out_specs=(hbm, hbm, hbm),
         scratch_shapes=[
             vmem((R, ROWS), F32),
             vmem((24, 128), I32),
@@ -437,10 +609,8 @@
             vmem((ROWS // 2, 128), F32),
             vmem((ROWS, 128), F32),
             vmem((DEV, HALF, 128), F32),
-            vmem((DEV, HALF, 128), F32),
-            vmem((2 * DEV * PITCH, 128), F32),
-            vmem((R, ROWS), F32),
-            vmem((LEVELS, R, W), F32),
+            vmem((LEVELS * R, W), F32),
+            vmem((R, W), F32),
             vmem((R, W), F32),
             vmem((LEAF, R, W), F32),
             vmem((12 * 128, 256), BF16),
@@ -450,11 +620,19 @@
             vmem((48, 128), I32),
             pltpu.SMEM((24, 128), I32),
             pltpu.SMEM((48, 128), I32),
-            pltpu.SMEM((24, 128), I32),
             pltpu.SemaphoreType.DMA((7,)),
             pltpu.SemaphoreType.DMA((4,)),
-            pltpu.SemaphoreType.DMA((LEVELS, 2)),
-            pltpu.SemaphoreType.DMA((LEVELS,)),
+            pltpu.SemaphoreType.DMA((2,)),
+            pltpu.SemaphoreType.DMA,
+            pltpu.SemaphoreType.DMA,
+            pltpu.SemaphoreType.DMA((2,)),
+            pltpu.SemaphoreType.DMA,
+            pltpu.SemaphoreType.DMA,
+            pltpu.SemaphoreType.DMA,
+            pltpu.SemaphoreType.DMA,
+            pltpu.SemaphoreType.DMA((3,)),
+            pltpu.SemaphoreType.DMA((3,)),
+            pltpu.SemaphoreType.DMA((3,)),
             pltpu.SemaphoreType.DMA,
             pltpu.SemaphoreType.DMA,
             pltpu.SemaphoreType.DMA,
@@ -472,8 +650,24 @@
         sep_parent[0],
         leaf_inverse[0],
         leaf_coupling[0].reshape(LEAF * NCOUP, W, W),
-        leaf_links[0],
+        leaf_links[0].T,
     )
+    x, sep = pl.pallas_call(
+        restore_kernel,
+        out_shape=(jax.ShapeDtypeStruct((R, ROWS), F32), jax.ShapeDtypeStruct((R, W), F32)),
+        in_specs=[hbm, pl.BlockSpec(memory_space=pltpu.SMEM), hbm],
+        out_specs=(hbm, hbm),
+        scratch_shapes=[
+            vmem((DEV, HALF, 128), F32),
+            vmem((2 * DEV * PITCH, 128), F32),
+            vmem((ROWS // 2, 128), F32),
+            vmem((R, ROWS), F32),
+            pltpu.SemaphoreType.DMA((2,)),
+            pltpu.SemaphoreType.DMA,
+        ],
+        compiler_params=pltpu.CompilerParams(vmem_limit_bytes=56 << 20),
+        name="restore_rows",
+    )(came, pos, sep)
     return x.T, sep.T[None]
 
 

time: 88.1 us -> 73.2 us (0.83)
  Pallas kernels: 82.3 us -> 72.3 us
  local copies, waits for them, and re-layouts: 4.9 us -> 0 us
    pallas_call x1 -> x2, Pallas kernels: 82.3 us -> 72.3 us  [the longest x1 64.7 us: per_device(): pl.pallas_call(kernel, out_shape=(jax.ShapeDtypeStruct((DEV, HALF, 128),...]
    unnamed x2 -> x0, local copies, waits for them, and re-layouts: 3.54 us -> none
    squeeze x1 -> x0, local copies, waits for them, and re-layouts: 1.36 us -> none  [per_device(): leaf_links[0]]
where the time goes in v2:
time: 73.2 us; the launch traced here: 73 us
  Pallas kernels  72.3 us (99%)
    pallas_call x1, Pallas kernels, per_device(): pl.pallas_call(kernel, out_shape=(jax.ShapeDtypeStruct((DEV, HALF, 128),...  64.7 us
    pallas_call x1, Pallas kernels, per_device(): pl.pallas_call(restore_kernel, out_shape=(jax.ShapeDtypeStruct((R, ROWS),...  7.61 us

profile of v2, /device:TPU:1, one launch (start us, length us, event | category | flops | bytes accessed | tf_op | source)
XLA Modules:
  0.0 73.0 jit_solution(2859775052383949157)
XLA Ops:
  0.6 64.7 %gmrf_solve.1 = (f32[128,12,128]{2,1,0:T(8,128)}, s32[24,128]{1,0:T(8,128)}, f32[64,256]{1,0:T(8,128)}) custom-call(f32[64,3072]{1,0:T(8,128)} %bitcast.18, s32[24,128]{1,0:T(8,128)} %bitcast.22, f32[64,256]{1,0:T(8,128)} %bitcast.21, f32[256,256]{1,0:T(8,128)} %bitcast.19, f32[256,256]{1,0:T(8,128)} %bitcast.20, f32[12,256,256]{2,1,0:T(8,128)} %bitcast.17, ...), custom_call_target="tpu_custom_call" | custom-call | tf_op jit(solution)/shard_map/gmrf_solve/pallas_call | solution.py:588
  65.4 7.6 %restore_rows.1 = (f32[64,3072]{1,0:T(8,128)}, f32[64,256]{1,0:T(8,128)}) custom-call(f32[128,12,128]{2,1,0:T(8,128)} %get-tuple-element.7.came_hbm, s32[24,128]{1,0:T(8,128)} %get-tuple-element.8.pos, f32[64,256]{1,0:T(8,128)} %get-tuple-element.9.sep_hbm), custom_call_target="tpu_custom_call" | custom-call | tf_op jit(solution)/shard_map/restore_rows/pallas_call | solution.py:655

commit v3 on v2

--- a/solution.py
+++ b/solution.py
@@ -24,8 +24,8 @@
 SEG = 24
 HALF = 12
 MSG = HALF + 1
-SPREAD = 37
-EARLY = (1, 1, 24, 64, 100)
+SPREAD = 11
+CUTS = 4
 PITCH = 16
 
 
@@ -70,46 +70,36 @@
     return total
 
 
-def gather_pairs(steps, source, table, second, store):
+def gather_pairs(steps, source, table, first, second, store, lanes=range(128)):
     left = iota((1, 128), 1) < R
 
     def step(k, carry):
-        for l in range(128):
+        for l in lanes:
             a = table[first(k), l]
             b = table[second(k), l]
             store(k, l, jnp.where(left, source[pl.ds(a, 1), :], source[pl.ds(b, 1), :]))
         return carry
 
-    first, second = second
     lax.fori_loop(0, steps, step, 0)
 
 
-def double_halves(value):
-    left = iota(value.shape, value.ndim - 1) < R
-    swapped = pltpu.roll(value, R, value.ndim - 1)
-    return jnp.where(left, value, swapped), jnp.where(left, swapped, value)
-
-
-def double_messages(src, dst, n):
+def swap_halves(both, first=0, count=DEV * PITCH):
     def group(g, carry):
-        lo2, hi2 = double_halves(src[pl.ds(g * 8, 8)])
-        for i in range(8):
-            at = pl.multiple_of((g * 8 + i) * PITCH, PITCH)
-            dst[pl.ds(at, n), :] = lo2[i]
-            dst[pl.ds(pl.multiple_of(at + DEV * PITCH, PITCH), n), :] = hi2[i]
+        at = pl.multiple_of(first + g * 128, 128)
+        both[pl.ds(at + DEV * PITCH, 128), :] = pltpu.roll(both[pl.ds(at, 128), :], R, 1)
         return carry
 
-    lax.fori_loop(0, DEV // 8, group, 0)
+    lax.fori_loop(0, count // 128, group, 0, unroll=2)
 
 
 def kernel(
     rhs_hbm, map_hbm, seprhs_hbm, sepinv_hbm, seppar_hbm, leafinv_hbm, coup_hbm, links,
     came_hbm, pos_hbm, sep_hbm,
     rhs, rmap, seprhs, sepinv, seppar, leafinv, coup,
-    doubled, sbuf, rbuf, received, grouped, solved, sbuf2,
-    anc, crit, sepout, acc, qt, cums, labels, pos_v, idx_v, idx, idx_r,
-    in_sem, loc_sem, crit_send, crit_recv, part_recv, zero_send, zero_recv, five_send, five_recv,
-    scat_send, scat_recv, ag_send, ag_recv, a_send, a_recv, b_send, b_recv,
+    doubled, sbuf, received, grouped, solved, sbuf2,
+    anc, crit, sepout, ready, acc, qt, cums, labels, pos_v, idx_v, idx, idx_r,
+    in_sem, loc_sem, crit_send, crit_recv, part_recv, zero_send, zero_recv, four_send, four_recv, five_send, five_recv,
+    scat_send, scat_recv, ag_send, ag_recv, a_send, a_recv, b_send, b_recv, gate,
 ):
     me = lax.axis_index("row") * 16 + lax.axis_index("col")
 
@@ -127,18 +117,8 @@
 
     barrier = pltpu.get_barrier_semaphore()
 
-    def greet(k):
+    for k in [16 * i for i in range(1, 8)] + list(range(1, 16)):
         pl.semaphore_signal(barrier, inc=1, device_id=mesh_id(me ^ k), device_id_type=MESH)
-
-    for k in range(1, 8):
-        greet(k)
-
-    def greet8(i, carry):
-        for k in range(8):
-            greet(i * 8 + k)
-        return carry
-
-    lax.fori_loop(1, DEV // 8, greet8, 0)
 
     own = 6 - trailing_zeros(me + 1)
     reach = lax.shift_right_logical(jnp.int32(32), jnp.clip(own, 0, 5))
@@ -160,11 +140,19 @@
     def set_level(m, value):
         anc[m * R:(m + 1) * R, :] = value
 
-    def to_children(act):
+    def to_children(act, cuts):
         @pl.when(inner)
         def _():
-            act(remote(sepout, crit, crit_send.at[0], crit_recv, me - reach))
-            act(remote(sepout, crit, crit_send.at[1], crit_recv, me + reach))
+            for i in range(cuts):
+                part = pl.ds(i * (R // cuts), R // cuts)
+                act(remote(sepout.at[part], crit.at[part], crit_send.at[0], crit_recv, me - reach))
+                act(remote(sepout.at[part], crit.at[part], crit_send.at[1], crit_recv, me + reach))
+
+    def start_children():
+        to_children(lambda c: c.start(), CUTS)
+
+    def finish_children():
+        to_children(lambda c: c.wait_send(), 1)
 
     def to_partner():
         return remote(sepout, rows_of(6 * R, R), crit_send.at[0], part_recv, me + 1)
@@ -172,17 +160,30 @@
     def zero_to(to, which):
         return remote(crit, rows_of(0, R), zero_send.at[which], zero_recv, to)
 
+    def four_to():
+        return [
+            remote(sepout, rows_of(4 * R, R), four_send.at[i], four_recv, (me & 120) | low)
+            for i, low in enumerate((0, 2, 7, 4, 6))
+        ]
+
     def five_to():
-        return remote(sepout, rows_of(5 * R, R), five_send, five_recv, me + 2)
+        return remote(crit, rows_of(5 * R, R), five_send, five_recv, me + 3)
 
     def finish_solve(target):
         t2, th = pieces(target)
         sepout[...] = dot3(t2, th, sepinv[...], NT)
 
     def take_and_solve():
-        pltpu.make_async_copy(sepout, crit, crit_recv).wait()
-        p2, ph = pieces(crit[...])
-        finish_solve(seprhs[...] - dot3(p2, ph, seppar[...], NN))
+        with jax.named_scope("parent_wait"):
+            pltpu.make_async_copy(sepout, crit, crit_recv).wait()
+
+        @pl.when((own == 6) & (x_at == 0))
+        def _():
+            five_to().start()
+
+        with jax.named_scope("own_solve"):
+            p2, ph = pieces(crit[...])
+            finish_solve(seprhs[...] - dot3(p2, ph, seppar[...], NN))
 
     loads[0].wait()
     loads[1].wait()
@@ -190,6 +191,15 @@
     @pl.when(own == 0)
     def _():
         finish_solve(seprhs[...])
+
+    pl.semaphore_wait(barrier, 22)
+
+    for i in range(1, 8):
+        pl.semaphore_signal(gate, inc=1, device_id=mesh_id(me ^ (16 * i)), device_id_type=MESH)
+
+    @pl.when(own == 0)
+    def _():
+        start_children()
 
     @pl.when(own < 0)
     def _():
@@ -232,7 +242,7 @@
                 )
             )
             at = dest[r:r + 1, :] * PITCH + rank + jnp.where(rank >= HALF, DEV * PITCH - HALF, 0)
-            pos_v[r:r + 1, :] = within(at, 2 * DEV * PITCH)
+            pos_v[r:r + 1, :] = within(at, 2 * DEV * PITCH) ^ (h * DEV * PITCH)
         digits = jnp.concatenate(parts, 1).astype(BF16)
         table = table + lax.dot_general(digits, qt[j * 128:(j + 1) * 128, :], NT, preferred_element_type=F32)
         carry = carry + cums[j * 128:(j + 1) * 128, 256:384]
@@ -256,49 +266,51 @@
     to_idx.wait()
 
     def put_send(k, l, row):
-        sbuf[l, pl.ds(k, 1), :] = row
-
-    gather_pairs(HALF, doubled, idx, (lambda k: k, lambda k: k + HALF), put_send)
-    for l in range(128):
-        sbuf[l, HALF:MSG, :] = labels[l:l + 1, :]
-
-    def exchange(src, dst, send, recv, first, last):
+        sbuf[pl.ds(l * PITCH + k, 1), :] = row
+
+    def landing(dst, device, n):
+        return dst.at[pl.ds(pl.multiple_of(device * PITCH, PITCH), n)]
+
+    def exchange(core, src, dst, n, send, recv):
         def go(k, carry):
-            to = me ^ ((k * SPREAD) & (DEV - 1))
-            remote(src.at[to], dst.at[me], send, recv, to).start()
+            j = (k * SPREAD) & 63
+            to = (me ^ ((j & 15) + (j // 16) * 32)) & 111 | (core * 16)
+
+            @pl.when(to != me)
+            def _():
+                remote(landing(src, to, n), landing(dst, me, n), send, recv, to).start()
+
             return carry
 
-        lax.fori_loop(first, last, go, 0)
-
-    def exchange_wait(src, dst, sem):
-        n = DEV - 1
-        pltpu.make_async_copy(src.at[pl.ds(0, n)], dst.at[pl.ds(0, n)], sem).wait()
-
-    keep = pltpu.make_async_copy(sbuf.at[me], rbuf.at[me], loc_sem.at[2])
-    keep.start()
+        lax.fori_loop(0, 64, go, 0)
+
+    def lanes_of(core):
+        return [l for l in range(DEV) if (l >> 4) & 1 == core]
+
+    def exchange_wait(rows, n, sem):
+        count = (DEV - 1) * n
+        pltpu.make_async_copy(rows.at[pl.ds(0, count)], rows.at[pl.ds(0, count)], sem).wait()
+
     loads[3].wait()
-    pl.semaphore_wait(barrier, DEV - 1)
+
+    pl.semaphore_wait(gate, 7)
 
     @pl.when(own == 0)
     def _():
-        to_children(lambda c: c.start())
+        finish_children()
+
+    @pl.when((own >= 1) & (own <= 2))
+    def _():
+        take_and_solve()
+        start_children()
 
     @pl.when(own == 1)
     def _():
-        take_and_solve()
-        to_children(lambda c: c.start())
+        finish_children()
         zero_to(me - reach, 0).start()
         zero_to(me + reach, 1).start()
-
-    early = jnp.int32(DEV)
-    for l, count in enumerate(EARLY):
-        early = jnp.where(own == l, count, early)
-    exchange(sbuf, rbuf, a_send, a_recv, 1, early)
-
-    @pl.when((own >= 2) & (own <= 4))
-    def _():
-        take_and_solve()
-        to_children(lambda c: c.start())
+        zero_to(me - reach, 0).wait_send()
+        zero_to(me + reach, 1).wait_send()
 
     @pl.when(own == 2)
     def _():
@@ -313,8 +325,18 @@
 
         lax.fori_loop(0, 24, tile, 0)
 
+    gather_pairs(HALF, doubled, idx, lambda k: k, lambda k: k + HALF, put_send)
+    for l in range(DEV):
+        sbuf[l * PITCH + HALF:l * PITCH + MSG, :] = labels[l:l + 1, :]
+    for core in range(2):
+        exchange(core, sbuf, received, MSG, a_send, a_recv)
+    keep = pltpu.make_async_copy(landing(sbuf, me, MSG), landing(received, me, MSG), loc_sem.at[2])
+    keep.start()
+
     @pl.when(own == 3)
     def _():
+        take_and_solve()
+        start_children()
         set_level(3, sepout[...])
         for i in range(8):
             part = rows_of(3 * R + 8 * i, 8)
@@ -322,12 +344,12 @@
 
     @pl.when(own == 4)
     def _():
+        take_and_solve()
+        start_children()
         set_level(4, sepout[...])
-        for i in range(4):
-            part = rows_of(4 * R + 16 * i, 16)
-            remote(part, part, scat_send, scat_recv.at[2], (me & 120) | (i // 2 * 4 + i % 2 * 2)).start()
-
-    exchange(sbuf, rbuf, a_send, a_recv, early, DEV)
+        finish_children()
+        for c in four_to():
+            c.start()
 
     @pl.when(x_at != 3)
     def _():
@@ -361,60 +383,10 @@
 
         lax.fori_loop(1, 16, hand, 0)
 
-    loads[5].wait()
-    acc[...] = jnp.zeros_like(acc)
-
-    def level(m, carry):
-        p = LEVELS - 1 - m
-        x2, xh = pieces(anc[pl.ds(pl.multiple_of(m * R, R), R), :])
-
-        def blocks(g, c0):
-            for u in range(4):
-                s = g * 4 + u
-                which = jnp.int32(0)
-                found = jnp.int32(0)
-                for c in range(NCOUP):
-                    here = jnp.where(links[c, s] == p, 1, 0)
-                    which = jnp.where(here > 0, c, which)
-                    found = found + here
-                term = dot3(x2, xh, coup[s * NCOUP + which], NN)
-                acc[s] += jnp.where(found > 0, term, 0.0)
-            return c0
-
-        lax.fori_loop(0, LEAF // 4, blocks, 0)
-        return carry
-
-    @pl.when((x_at != 3))
-    def _():
-        drain(184, ag_recv.at[0])
-
-    @pl.when((x_at == 3) & (own != 2))
-    def _():
-        drain(192, ag_recv.at[0])
-
-    lax.fori_loop(0, 3, level, 0)
-
-    @pl.when(own == 5)
-    def _():
-        take_and_solve()
-        to_children(lambda c: c.start())
-        five_to().start()
-        set_level(4, crit[...])
-        set_level(5, sepout[...])
-
-    @pl.when(even)
-    def _():
-        drain(16, scat_recv.at[2])
-        part = rows_of(4 * R + (lax.shift_right_logical(me, 2) & 1) * 32 + x_at * 8, 16)
-        for low in (0, 2, 4, 6, 7):
-            @pl.when((me & 7) != low)
-            def _():
-                remote(part, part, ag_send.at[2], ag_recv.at[2], (me & 120) | low).start()
-
-    exchange_wait(sbuf, rbuf, a_recv)
+    exchange_wait(doubled, MSG, a_recv)
     keep.wait()
     for p in range(128):
-        labels[p:p + 1, :] = rbuf[p, HALF:MSG, :]
+        labels[p:p + 1, :] = received[p * PITCH + HALF:p * PITCH + MSG, :]
     got = labels[...].T[0:32].astype(I32)
     high = lax.shift_right_logical(got, 7)
     low = got & 127
@@ -438,18 +410,27 @@
         inverse = inverse + lax.dot_general(
             jnp.concatenate(aa, 1).astype(BF16), jnp.concatenate(bb, 1).astype(BF16), NT, preferred_element_type=F32
         )
-    idx_v[0:24, :] = within((inverse[0:24] * 64.0 + inverse[32:56]).astype(I32), 2 * DEV * PITCH)
+    found_at = within((inverse[0:24] * 64.0 + inverse[32:56]).astype(I32), 2 * DEV * PITCH)
+    idx_v[0:24, :] = found_at ^ ((iota((24, 128), 0) & 1) * (DEV * PITCH))
     idx_v[24:48, :] = within(((high & 1) * (ROWS // 2) + lax.shift_right_logical(high, 1) * 128 + low)[0:24], ROWS)
     to_idx = pltpu.make_async_copy(idx_v, idx_r, loc_sem.at[0])
     to_idx.start()
 
-    double_messages(rbuf, received, MSG)
+    swap_halves(received)
+    @pl.when(own == 5)
+    def _():
+        take_and_solve()
+        start_children()
+        set_level(4, crit[...])
+        set_level(5, sepout[...])
+        finish_children()
+
     to_idx.wait()
 
     def put_grouped(k, l, row):
         grouped[pl.ds(k * 128 + l, 1), :] = row
 
-    gather_pairs(LEAF, received, idx_r, (lambda k: 2 * k, lambda k: 2 * k + 1), put_grouped)
+    gather_pairs(LEAF, received, idx_r, lambda k: 2 * k, lambda k: 2 * k + 1, put_grouped)
 
     @pl.when(own == 6)
     def _():
@@ -458,32 +439,73 @@
         set_level(5, crit[...])
         set_level(6, sepout[...])
 
+    loads[5].wait()
+
+    def make_ready(m):
+        x2, _ = pieces(anc[m * R:(m + 1) * R, :])
+        ready[m] = x2
+
+    def block(i):
+        def blocks(g, carry):
+            for u in range(4):
+                s = g * 4 + u
+                link = [links[c, s] for c in range(NCOUP)]
+                which = jnp.int32(0)
+                level = jnp.int32(0)
+                for c in range(NCOUP):
+                    above = jnp.int32(0)
+                    for other in range(NCOUP):
+                        if other != c:
+                            above = above + jnp.where(link[other] > link[c], 1, 0)
+                    which = jnp.where(above == i, c, which)
+                    level = jnp.where(above == i, LEVELS - 1 - link[c], level)
+                x2 = ready[level]
+                term = dot3(x2, x2[:R], coup[s * NCOUP + which], NN)
+                acc[s] = term if i == 0 else acc[s] + term
+            return carry
+
+        lax.fori_loop(0, LEAF // 4, blocks, 0)
+
+    @pl.when((x_at != 3))
+    def _():
+        drain(184, ag_recv.at[0])
+
+    @pl.when((x_at == 3) & (own != 2))
+    def _():
+        drain(192, ag_recv.at[0])
+
     @pl.when(even)
     def _():
         drain(56, ag_recv.at[1])
-        drain(48, ag_recv.at[2])
 
     @pl.when(~even & ((me & 15) != 7))
     def _():
         drain(64, ag_recv.at[1])
 
-    @pl.when((me & 7) == 7)
-    def _():
-        drain(64, ag_recv.at[2])
-
-    lax.fori_loop(3, 5, level, 0)
+    for m in range(4):
+        make_ready(m)
+    block(0)
+
+    @pl.when(even | ((me & 7) == 7))
+    def _():
+        drain(R, four_recv)
+
+    make_ready(4)
+    block(1)
 
     @pl.when(x_at == 3)
     def _():
         drain(R, five_recv)
 
-    lax.fori_loop(5, 6, level, 0)
+    make_ready(5)
+    block(2)
 
     @pl.when(~even)
     def _():
         drain(R, part_recv)
 
-    lax.fori_loop(6, 7, level, 0)
+    make_ready(6)
+    block(3)
 
     loads[6].wait()
 
@@ -502,39 +524,43 @@
     lax.fori_loop(0, LEAF // 4, leaf, 0)
 
     def put_back(k, l, row):
-        sbuf2[l, pl.ds(k, 1), :] = row
-
-    gather_pairs(HALF, solved, idx_r, (lambda k: k + 24, lambda k: k + 24 + HALF), put_back)
-    mine = pltpu.make_async_copy(sbuf2.at[me], came_hbm.at[me], loc_sem.at[2])
+        sbuf2[pl.ds(l * PITCH + k, 1), :] = row
+
+    for core in range(2):
+        gather_pairs(HALF, solved, idx_r, lambda k: k + 24, lambda k: k + 24 + HALF, put_back, lanes_of(core))
+        exchange(core, sbuf2, came_hbm, HALF, b_send, b_recv)
+    mine = pltpu.make_async_copy(landing(sbuf2, me, HALF), landing(came_hbm, me, HALF), loc_sem.at[2])
     mine.start()
-    exchange(sbuf2, came_hbm, b_send, b_recv, 1, DEV)
     out_sep = pltpu.make_async_copy(sepout, sep_hbm, loc_sem.at[3])
     out_sep.start()
 
-    exchange_wait(sbuf, rbuf, a_send)
-    to_children(lambda c: c.wait_send())
+    exchange_wait(doubled, MSG, a_send)
 
     @pl.when(own == 6)
     def _():
         to_partner().wait_send()
 
-    @pl.when(own == 5)
+    @pl.when(x_at == 0)
     def _():
         five_to().wait_send()
 
-    @pl.when(own == 1)
-    def _():
-        zero_to(me - reach, 0).wait_send()
-        zero_to(me + reach, 1).wait_send()
+    @pl.when((own == 2) | (own == 3))
+    def _():
+        finish_children()
 
     @pl.when(own == 2)
     def _():
         drain(192, scat_send)
 
-    @pl.when((own == 3) | (own == 4))
+    @pl.when(own == 3)
     def _():
         drain(64, scat_send)
 
+    @pl.when(own == 4)
+    def _():
+        for c in four_to():
+            c.wait_send()
+
     @pl.when(x_at != 3)
     def _():
         drain(240, ag_send.at[0])
@@ -542,44 +568,58 @@
     @pl.when(even)
     def _():
         drain(112, ag_send.at[1])
-        drain(64, ag_send.at[2])
 
     to_pos.wait()
     out_sep.wait()
     mine.wait()
-    exchange_wait(sbuf2, came_hbm, b_recv)
-    exchange_wait(sbuf2, came_hbm, b_send)
-
-
-def restore_kernel(came_hbm, pos, sep_hbm, x_hbm, sepx_hbm, came, returned, grouped, xout, sem, out_sem):
-    load = pltpu.make_async_copy(came_hbm, came, sem.at[0])
-    load.start()
+    exchange_wait(doubled, HALF, b_recv)
+    exchange_wait(doubled, HALF, b_send)
+
+
+def restore_kernel(came_hbm, pos, sep_hbm, x_hbm, sepx_hbm, came, grouped, xout, sem, out_sem):
+    part = DEV * PITCH // 4
+    loads = [
+        pltpu.make_async_copy(came_hbm.at[pl.ds(i * part, part)], came.at[pl.ds(i * part, part)], sem.at[2 + i])
+        for i in range(4)
+    ]
+    for load in loads:
+        load.start()
     move = pltpu.make_async_copy(sep_hbm, sepx_hbm, sem.at[1])
     move.start()
-    load.wait()
-    double_messages(came, returned, HALF)
+    with jax.named_scope("load_and_swap"):
+        for i in range(4):
+            loads[i].wait()
+            swap_halves(came, i * part, part)
     left = iota((1, 128), 1) < R
 
-    def put(j):
-        return pltpu.make_async_copy(
-            xout.at[:, pl.ds(pl.multiple_of(j * 256, 256), 256)],
-            x_hbm.at[:, pl.ds(pl.multiple_of(j * 256, 256), 256)],
-            out_sem,
-        )
-
-    def restore(j, carry):
+    def pick(j, slot):
         for l in range(128):
             a = pos[2 * j, l]
             b = pos[2 * j + 1, l]
-            grouped[pl.ds(j * 128 + l, 1), :] = jnp.where(left, returned[pl.ds(a, 1), :], returned[pl.ds(b, 1), :])
-        both = grouped[pl.ds(pl.multiple_of(j * 128, 128), 128), :].T
-        xout[:, pl.ds(pl.multiple_of(j * 256, 256), 256)] = jnp.concatenate([both[:R], both[R:]], 1)
-        put(j).start()
+            grouped[slot, l:l + 1, :] = jnp.where(left, came[pl.ds(a, 1), :], came[pl.ds(b, 1), :])
+
+    def write(j, slot):
+        at = pl.ds(pl.multiple_of(j * 256, 256), 256)
+        both = grouped[slot].T
+        xout[:, at] = jnp.concatenate([both[:R], both[R:]], 1)
+        pltpu.make_async_copy(xout.at[:, at], x_hbm.at[:, at], out_sem).start()
+
+    with jax.named_scope("pick_first"):
+        pick(0, 0)
+
+    def step(i, carry):
+        j = 2 * i
+        pick(j + 1, 1)
+        write(j, 0)
+        pick(jnp.minimum(j + 2, LEAF - 1), 0)
+        write(j + 1, 1)
         return carry
 
-    lax.fori_loop(0, LEAF, restore, 0)
-    pltpu.make_async_copy(xout, x_hbm, out_sem).wait()
-    move.wait()
+    with jax.named_scope("pick_and_write"):
+        lax.fori_loop(0, LEAF // 2, step, 0)
+    with jax.named_scope("drain"):
+        pltpu.make_async_copy(xout, x_hbm, out_sem).wait()
+        move.wait()
 
 
 def per_device(rhs_held, row_map, sep_rhs, sep_inverse, sep_parent, leaf_inverse, leaf_coupling, leaf_links):
@@ -588,7 +628,7 @@
     came, pos, sep = pl.pallas_call(
         kernel,
         out_shape=(
-            jax.ShapeDtypeStruct((DEV, HALF, 128), F32),
+            jax.ShapeDtypeStruct((DEV * PITCH, 128), F32),
             jax.ShapeDtypeStruct((24, 128), I32),
             jax.ShapeDtypeStruct((R, W), F32),
         ),
@@ -603,15 +643,15 @@
             vmem((LEAF, W, W), F32),
             vmem((LEAF * NCOUP, W, W), F32),
             vmem((ROWS, 128), F32),
-            vmem((DEV, MSG, 128), F32),
-            vmem((DEV, MSG, 128), F32),
+            vmem((DEV * PITCH, 128), F32),
             vmem((2 * DEV * PITCH, 128), F32),
             vmem((ROWS // 2, 128), F32),
             vmem((ROWS, 128), F32),
-            vmem((DEV, HALF, 128), F32),
+            vmem((DEV * PITCH, 128), F32),
             vmem((LEVELS * R, W), F32),
             vmem((R, W), F32),
             vmem((R, W), F32),
+            vmem((LEVELS, 2 * R, W), BF16),
             vmem((LEAF, R, W), F32),
             vmem((12 * 128, 256), BF16),
             vmem((12 * 128, 384), F32),
@@ -627,16 +667,19 @@
             pltpu.SemaphoreType.DMA,
             pltpu.SemaphoreType.DMA((2,)),
             pltpu.SemaphoreType.DMA,
-            pltpu.SemaphoreType.DMA,
-            pltpu.SemaphoreType.DMA,
-            pltpu.SemaphoreType.DMA,
-            pltpu.SemaphoreType.DMA((3,)),
-            pltpu.SemaphoreType.DMA((3,)),
-            pltpu.SemaphoreType.DMA((3,)),
-            pltpu.SemaphoreType.DMA,
-            pltpu.SemaphoreType.DMA,
-            pltpu.SemaphoreType.DMA,
-            pltpu.SemaphoreType.DMA,
+            pltpu.SemaphoreType.DMA((5,)),
+            pltpu.SemaphoreType.DMA,
+            pltpu.SemaphoreType.DMA,
+            pltpu.SemaphoreType.DMA,
+            pltpu.SemaphoreType.DMA,
+            pltpu.SemaphoreType.DMA((2,)),
+            pltpu.SemaphoreType.DMA((2,)),
+            pltpu.SemaphoreType.DMA((2,)),
+            pltpu.SemaphoreType.DMA,
+            pltpu.SemaphoreType.DMA,
+            pltpu.SemaphoreType.DMA,
+            pltpu.SemaphoreType.DMA,
+            pltpu.SemaphoreType.REGULAR,
         ],
         compiler_params=pltpu.CompilerParams(
             collective_id=0, has_side_effects=True, vmem_limit_bytes=56 << 20
@@ -658,11 +701,10 @@
         in_specs=[hbm, pl.BlockSpec(memory_space=pltpu.SMEM), hbm],
         out_specs=(hbm, hbm),
         scratch_shapes=[
-            vmem((DEV, HALF, 128), F32),
             vmem((2 * DEV * PITCH, 128), F32),
-            vmem((ROWS // 2, 128), F32),
+            vmem((2, 128, 128), F32),
             vmem((R, ROWS), F32),
-            pltpu.SemaphoreType.DMA((2,)),
+            pltpu.SemaphoreType.DMA((6,)),
             pltpu.SemaphoreType.DMA,
         ],
         compiler_params=pltpu.CompilerParams(vmem_limit_bytes=56 << 20),

time: 73.2 us -> 66.5 us (0.908)
  Pallas kernels: 72.3 us -> 65.7 us
    pallas_call x1, Pallas kernels: 64.7 us -> 59.1 us  [per_device(): pl.pallas_call(kernel, out_shape=(jax.ShapeDtypeStruct((DEV * PITCH, 128)...]
    pallas_call x1, Pallas kernels: 7.61 us -> 6.51 us  [per_device(): pl.pallas_call(restore_kernel, out_shape=(jax.ShapeDtypeStruct((R, ROWS),...]
where the time goes in v3:
time: 66.5 us; the launch traced here: 66.3 us
  Pallas kernels  65.7 us (99%)
    pallas_call x1, Pallas kernels, per_device(): pl.pallas_call(kernel, out_shape=(jax.ShapeDtypeStruct((DEV * PITCH, 128)...  59.1 us
    pallas_call x1, Pallas kernels, per_device(): pl.pallas_call(restore_kernel, out_shape=(jax.ShapeDtypeStruct((R, ROWS),...  6.51 us

profile of v3, /device:TPU:1, one launch (start us, length us, event | category | flops | bytes accessed | tf_op | source)
XLA Modules:
  0.0 66.3 jit_solution(16024048192322066184)
XLA Ops:
  0.6 59.1 %gmrf_solve.1 = (f32[2048,128]{1,0:T(8,128)}, s32[24,128]{1,0:T(8,128)}, f32[64,256]{1,0:T(8,128)}) custom-call(f32[64,3072]{1,0:T(8,128)} %bitcast.18, s32[24,128]{1,0:T(8,128)} %bitcast.22, f32[64,256]{1,0:T(8,128)} %bitcast.21, f32[256,256]{1,0:T(8,128)} %bitcast.19, f32[256,256]{1,0:T(8,128)} %bitcast.20, f32[12,256,256]{2,1,0:T(8,128)} %bitcast.17, ...), custom_call_target="tpu_custom_call" | custom-call | tf_op jit(solution)/shard_map/gmrf_solve/pallas_call | solution.py:628
  59.8 6.5 %restore_rows.1 = (f32[64,3072]{1,0:T(8,128)}, f32[64,256]{1,0:T(8,128)}) custom-call(f32[2048,128]{1,0:T(8,128)} %get-tuple-element.7.came_hbm, s32[24,128]{1,0:T(8,128)} %get-tuple-element.8.pos, f32[64,256]{1,0:T(8,128)} %get-tuple-element.9.sep_hbm), custom_call_target="tpu_custom_call" | custom-call | tf_op jit(solution)/shard_map/restore_rows/pallas_call | solution.py:698

commit v4 on v3

--- a/solution.py
+++ b/solution.py
@@ -24,8 +24,9 @@
 SEG = 24
 HALF = 12
 MSG = HALF + 1
-SPREAD = 11
-CUTS = 4
+SPREAD = 37
+PARTS = 4
+PART = R // PARTS
 PITCH = 16
 
 
@@ -140,22 +141,21 @@
     def set_level(m, value):
         anc[m * R:(m + 1) * R, :] = value
 
-    def to_children(act, cuts):
+    def send_part(h):
+        part = pl.ds(h * PART, PART)
+
         @pl.when(inner)
         def _():
-            for i in range(cuts):
-                part = pl.ds(i * (R // cuts), R // cuts)
-                act(remote(sepout.at[part], crit.at[part], crit_send.at[0], crit_recv, me - reach))
-                act(remote(sepout.at[part], crit.at[part], crit_send.at[1], crit_recv, me + reach))
-
-    def start_children():
-        to_children(lambda c: c.start(), CUTS)
+            remote(sepout.at[part], crit.at[part], crit_send.at[0], crit_recv.at[h], me - reach).start()
+            remote(sepout.at[part], crit.at[part], crit_send.at[1], crit_recv.at[h], me + reach).start()
+
+        @pl.when(own == 6)
+        def _():
+            remote(sepout.at[part], rows_of(6 * R + h * PART, PART), crit_send.at[0], part_recv, me + 1).start()
 
     def finish_children():
-        to_children(lambda c: c.wait_send(), 1)
-
-    def to_partner():
-        return remote(sepout, rows_of(6 * R, R), crit_send.at[0], part_recv, me + 1)
+        drain(R, crit_send.at[0])
+        drain(R, crit_send.at[1])
 
     def zero_to(to, which):
         return remote(crit, rows_of(0, R), zero_send.at[which], zero_recv, to)
@@ -167,39 +167,42 @@
         ]
 
     def five_to():
-        return remote(crit, rows_of(5 * R, R), five_send, five_recv, me + 3)
-
-    def finish_solve(target):
+        return remote(sepout, rows_of(5 * R, R), five_send, five_recv, me + 2)
+
+    def solve_part(h, target):
         t2, th = pieces(target)
-        sepout[...] = dot3(t2, th, sepinv[...], NT)
+        sepout[h * PART:(h + 1) * PART, :] = dot3(t2, th, sepinv[...], NT)
 
     def take_and_solve():
-        with jax.named_scope("parent_wait"):
-            pltpu.make_async_copy(sepout, crit, crit_recv).wait()
-
-        @pl.when((own == 6) & (x_at == 0))
+        for h in range(PARTS):
+            rows = slice(h * PART, (h + 1) * PART)
+            with jax.named_scope("parent_wait"):
+                pltpu.make_async_copy(sepout.at[pl.ds(0, PART)], crit.at[pl.ds(0, PART)], crit_recv.at[h]).wait()
+            with jax.named_scope("own_solve"):
+                p2, ph = pieces(crit[rows, :])
+                solve_part(h, seprhs[rows, :] - dot3(p2, ph, seppar[...], NN))
+            send_part(h)
+
+        @pl.when(own == 5)
         def _():
             five_to().start()
 
-        with jax.named_scope("own_solve"):
-            p2, ph = pieces(crit[...])
-            finish_solve(seprhs[...] - dot3(p2, ph, seppar[...], NN))
+    def heard_first():
+        pl.semaphore_wait(barrier, 22)
+
+        for i in range(1, 8):
+            pl.semaphore_signal(gate, inc=1, device_id=mesh_id(me ^ (16 * i)), device_id_type=MESH)
 
     loads[0].wait()
     loads[1].wait()
 
     @pl.when(own == 0)
     def _():
-        finish_solve(seprhs[...])
-
-    pl.semaphore_wait(barrier, 22)
-
-    for i in range(1, 8):
-        pl.semaphore_signal(gate, inc=1, device_id=mesh_id(me ^ (16 * i)), device_id_type=MESH)
-
-    @pl.when(own == 0)
-    def _():
-        start_children()
+        for h in range(PARTS):
+            solve_part(h, seprhs[h * PART:(h + 1) * PART, :])
+        heard_first()
+        for h in range(PARTS):
+            send_part(h)
 
     @pl.when(own < 0)
     def _():
@@ -291,26 +294,30 @@
         count = (DEV - 1) * n
         pltpu.make_async_copy(rows.at[pl.ds(0, count)], rows.at[pl.ds(0, count)], sem).wait()
 
+    @pl.when(own != 0)
+    def _():
+        heard_first()
+
     loads[3].wait()
 
-    pl.semaphore_wait(gate, 7)
-
-    @pl.when(own == 0)
-    def _():
-        finish_children()
-
-    @pl.when((own >= 1) & (own <= 2))
+    @pl.when(own == 1)
     def _():
         take_and_solve()
-        start_children()
-
-    @pl.when(own == 1)
-    def _():
-        finish_children()
         zero_to(me - reach, 0).start()
         zero_to(me + reach, 1).start()
-        zero_to(me - reach, 0).wait_send()
-        zero_to(me + reach, 1).wait_send()
+
+    gather_pairs(HALF, doubled, idx, lambda k: k, lambda k: k + HALF, put_send)
+    for l in range(DEV):
+        sbuf[l * PITCH + HALF:l * PITCH + MSG, :] = labels[l:l + 1, :]
+    pl.semaphore_wait(gate, 7)
+
+    @pl.when(own == 0)
+    def _():
+        finish_children()
+
+    @pl.when(own == 2)
+    def _():
+        take_and_solve()
 
     @pl.when(own == 2)
     def _():
@@ -325,9 +332,6 @@
 
         lax.fori_loop(0, 24, tile, 0)
 
-    gather_pairs(HALF, doubled, idx, lambda k: k, lambda k: k + HALF, put_send)
-    for l in range(DEV):
-        sbuf[l * PITCH + HALF:l * PITCH + MSG, :] = labels[l:l + 1, :]
     for core in range(2):
         exchange(core, sbuf, received, MSG, a_send, a_recv)
     keep = pltpu.make_async_copy(landing(sbuf, me, MSG), landing(received, me, MSG), loc_sem.at[2])
@@ -336,7 +340,6 @@
     @pl.when(own == 3)
     def _():
         take_and_solve()
-        start_children()
         set_level(3, sepout[...])
         for i in range(8):
             part = rows_of(3 * R + 8 * i, 8)
@@ -345,7 +348,6 @@
     @pl.when(own == 4)
     def _():
         take_and_solve()
-        start_children()
         set_level(4, sepout[...])
         finish_children()
         for c in four_to():
@@ -420,10 +422,8 @@
     @pl.when(own == 5)
     def _():
         take_and_solve()
-        start_children()
         set_level(4, crit[...])
         set_level(5, sepout[...])
-        finish_children()
 
     to_idx.wait()
 
@@ -435,7 +435,6 @@
     @pl.when(own == 6)
     def _():
         take_and_solve()
-        to_partner().start()
         set_level(5, crit[...])
         set_level(6, sepout[...])
 
@@ -538,15 +537,20 @@
 
     @pl.when(own == 6)
     def _():
-        to_partner().wait_send()
-
-    @pl.when(x_at == 0)
+        drain(R, crit_send.at[0])
+
+    @pl.when(own == 5)
     def _():
         five_to().wait_send()
 
-    @pl.when((own == 2) | (own == 3))
+    @pl.when(((own >= 1) & (own <= 3)) | (own == 5))
     def _():
         finish_children()
+
+    @pl.when(own == 1)
+    def _():
+        zero_to(me - reach, 0).wait_send()
+        zero_to(me + reach, 1).wait_send()
 
     @pl.when(own == 2)
     def _():
@@ -663,7 +667,7 @@
             pltpu.SemaphoreType.DMA((7,)),
             pltpu.SemaphoreType.DMA((4,)),
             pltpu.SemaphoreType.DMA((2,)),
-            pltpu.SemaphoreType.DMA,
+            pltpu.SemaphoreType.DMA((PARTS,)),
             pltpu.SemaphoreType.DMA,
             pltpu.SemaphoreType.DMA((2,)),
             pltpu.SemaphoreType.DMA,

time: 66.5 us -> 61.3 us (0.922)
  Pallas kernels: 65.7 us -> 60.4 us
    pallas_call x1, Pallas kernels: 59.1 us -> 53.9 us  [per_device(): pl.pallas_call(kernel, out_shape=(jax.ShapeDtypeStruct((DEV * PITCH, 128)...]
where the time goes in v4:
time: 61.3 us; the launch traced here: 61.1 us
  Pallas kernels  60.4 us (99%)
  between operations  0.64 us (1%)
    pallas_call x1, Pallas kernels, per_device(): pl.pallas_call(kernel, out_shape=(jax.ShapeDtypeStruct((DEV * PITCH, 128)...  53.9 us
    pallas_call x1, Pallas kernels, per_device(): pl.pallas_call(restore_kernel, out_shape=(jax.ShapeDtypeStruct((R, ROWS),...  6.51 us

profile of v4, /device:TPU:1, one launch (start us, length us, event | category | flops | bytes accessed | tf_op | source)
XLA Modules:
  0.0 61.1 jit_solution(6827363315132580207)
XLA Ops:
  0.6 53.9 %gmrf_solve.1 = (f32[2048,128]{1,0:T(8,128)}, s32[24,128]{1,0:T(8,128)}, f32[64,256]{1,0:T(8,128)}) custom-call(f32[64,3072]{1,0:T(8,128)} %bitcast.18, s32[24,128]{1,0:T(8,128)} %bitcast.22, f32[64,256]{1,0:T(8,128)} %bitcast.21, f32[256,256]{1,0:T(8,128)} %bitcast.19, f32[256,256]{1,0:T(8,128)} %bitcast.20, f32[12,256,256]{2,1,0:T(8,128)} %bitcast.17, ...), custom_call_target="tpu_custom_call" | custom-call | tf_op jit(solution)/shard_map/gmrf_solve/pallas_call | solution.py:632
  54.6 6.5 %restore_rows.1 = (f32[64,3072]{1,0:T(8,128)}, f32[64,256]{1,0:T(8,128)}) custom-call(f32[2048,128]{1,0:T(8,128)} %get-tuple-element.7.came_hbm, s32[24,128]{1,0:T(8,128)} %get-tuple-element.8.pos, f32[64,256]{1,0:T(8,128)} %get-tuple-element.9.sep_hbm), custom_call_target="tpu_custom_call" | custom-call | tf_op jit(solution)/shard_map/restore_rows/pallas_call | solution.py:702

commit v5 on v4

--- a/solution.py
+++ b/solution.py
@@ -24,6 +24,8 @@
 SEG = 24
 HALF = 12
 MSG = HALF + 1
+BLOCK_STEP = 12
+LEAF_STEP = 12
 SPREAD = 37
 PARTS = 4
 PART = R // PARTS
@@ -90,7 +92,7 @@
         both[pl.ds(at + DEV * PITCH, 128), :] = pltpu.roll(both[pl.ds(at, 128), :], R, 1)
         return carry
 
-    lax.fori_loop(0, count // 128, group, 0, unroll=2)
+    lax.fori_loop(0, count // 128, group, 0, unroll=4)
 
 
 def kernel(
@@ -264,7 +266,7 @@
         doubled[pl.ds(pl.multiple_of(j * 128, 128), 128), :] = jnp.concatenate([block, block], 0).T
         return carry
 
-    lax.fori_loop(0, ROWS // 128, double_rhs, 0, unroll=4)
+    lax.fori_loop(0, ROWS // 128, double_rhs, 0, unroll=12)
 
     to_idx.wait()
 
@@ -446,8 +448,8 @@
 
     def block(i):
         def blocks(g, carry):
-            for u in range(4):
-                s = g * 4 + u
+            for u in range(BLOCK_STEP):
+                s = g * BLOCK_STEP + u
                 link = [links[c, s] for c in range(NCOUP)]
                 which = jnp.int32(0)
                 level = jnp.int32(0)
@@ -463,7 +465,7 @@
                 acc[s] = term if i == 0 else acc[s] + term
             return carry
 
-        lax.fori_loop(0, LEAF // 4, blocks, 0)
+        lax.fori_loop(0, LEAF // BLOCK_STEP, blocks, 0)
 
     @pl.when((x_at != 3))
     def _():
@@ -509,8 +511,8 @@
     loads[6].wait()
 
     def leaf(g, carry):
-        for u in range(4):
-            t = g * 4 + u
+        for u in range(LEAF_STEP):
+            t = g * LEAF_STEP + u
             at = pl.multiple_of(t * 128, 128)
             both = grouped[pl.ds(at, 128), :].T
             target = jnp.concatenate([both[:R], both[R:]], 1) - acc[t]
@@ -520,7 +522,7 @@
             solved[pl.ds(pl.multiple_of(at + ROWS // 2, 128), 128), :] = jnp.concatenate([x[:, 128:], x[:, 128:]], 0).T
         return carry
 
-    lax.fori_loop(0, LEAF // 4, leaf, 0)
+    lax.fori_loop(0, LEAF // LEAF_STEP, leaf, 0)
 
     def put_back(k, l, row):
         sbuf2[pl.ds(l * PITCH + k, 1), :] = row

time: 61.3 us -> 59.3 us (0.967)
  Pallas kernels: 60.4 us -> 58.4 us
    pallas_call x1, Pallas kernels: 53.9 us -> 52.2 us  [per_device(): pl.pallas_call(kernel, out_shape=(jax.ShapeDtypeStruct((DEV * PITCH, 128)...]
where the time goes in v5:
time: 59.3 us; the launch traced here: 59.1 us
  Pallas kernels  58.4 us (98%)
  between operations  0.64 us (1%)
    pallas_call x1, Pallas kernels, per_device(): pl.pallas_call(kernel, out_shape=(jax.ShapeDtypeStruct((DEV * PITCH, 128)...  52.2 us
    pallas_call x1, Pallas kernels, per_device(): pl.pallas_call(restore_kernel, out_shape=(jax.ShapeDtypeStruct((R, ROWS),...  6.24 us

profile of v5, /device:TPU:1, one launch (start us, length us, event | category | flops | bytes accessed | tf_op | source)
XLA Modules:
  0.0 59.1 jit_solution(5285354706782263206)
XLA Ops:
  0.6 52.2 %gmrf_solve.1 = (f32[2048,128]{1,0:T(8,128)}, s32[24,128]{1,0:T(8,128)}, f32[64,256]{1,0:T(8,128)}) custom-call(f32[64,3072]{1,0:T(8,128)} %bitcast.18, s32[24,128]{1,0:T(8,128)} %bitcast.22, f32[64,256]{1,0:T(8,128)} %bitcast.21, f32[256,256]{1,0:T(8,128)} %bitcast.19, f32[256,256]{1,0:T(8,128)} %bitcast.20, f32[12,256,256]{2,1,0:T(8,128)} %bitcast.17, ...), custom_call_target="tpu_custom_call" | custom-call | tf_op jit(solution)/shard_map/gmrf_solve/pallas_call | solution.py:634
  52.8 6.2 %restore_rows.1 = (f32[64,3072]{1,0:T(8,128)}, f32[64,256]{1,0:T(8,128)}) custom-call(f32[2048,128]{1,0:T(8,128)} %get-tuple-element.7.came_hbm, s32[24,128]{1,0:T(8,128)} %get-tuple-element.8.pos, f32[64,256]{1,0:T(8,128)} %get-tuple-element.9.sep_hbm), custom_call_target="tpu_custom_call" | custom-call | tf_op jit(solution)/shard_map/restore_rows/pallas_call | solution.py:704

commit v6 on v5

--- a/solution.py
+++ b/solution.py
@@ -277,17 +277,20 @@
         return dst.at[pl.ds(pl.multiple_of(device * PITCH, PITCH), n)]
 
     def exchange(core, src, dst, n, send, recv):
-        def go(k, carry):
+        def send_one(k):
             j = (k * SPREAD) & 63
             to = (me ^ ((j & 15) + (j // 16) * 32)) & 111 | (core * 16)
-
-            @pl.when(to != me)
-            def _():
-                remote(landing(src, to, n), landing(dst, me, n), send, recv, to).start()
-
+            remote(landing(src, to, n), landing(dst, me, n), send, recv, to).start()
+
+        @pl.when((lax.shift_right_logical(me, 4) & 1) != core)
+        def _():
+            send_one(0)
+
+        def go(k, carry):
+            send_one(k)
             return carry
 
-        lax.fori_loop(0, 64, go, 0)
+        lax.fori_loop(1, 64, go, 0, unroll=1)
 
     def lanes_of(core):
         return [l for l in range(DEV) if (l >> 4) & 1 == core]
@@ -370,22 +373,6 @@
             return carry
 
         lax.fori_loop(1, 32, hand, 0)
-
-    @pl.when(even)
-    def _():
-        drain(8, scat_recv.at[1])
-        part = rows_of(3 * R + (lax.shift_right_logical(me, 2) & 3) * 16 + x_at * 4, 8)
-
-        def hand(k, carry):
-            to = me ^ k
-
-            @pl.when((to & 15) != 7)
-            def _():
-                remote(part, part, ag_send.at[1], ag_recv.at[1], to).start()
-
-            return carry
-
-        lax.fori_loop(1, 16, hand, 0)
 
     exchange_wait(doubled, MSG, a_recv)
     keep.wait()
@@ -426,6 +413,22 @@
         take_and_solve()
         set_level(4, crit[...])
         set_level(5, sepout[...])
+
+    @pl.when(even)
+    def _():
+        drain(8, scat_recv.at[1])
+        part = rows_of(3 * R + (lax.shift_right_logical(me, 2) & 3) * 16 + x_at * 4, 8)
+
+        def hand(k, carry):
+            to = me ^ k
+
+            @pl.when((to & 15) != 7)
+            def _():
+                remote(part, part, ag_send.at[1], ag_recv.at[1], to).start()
+
+            return carry
+
+        lax.fori_loop(1, 16, hand, 0)
 
     to_idx.wait()
 

time: 59.3 us -> 59.2 us (level)
  no operation moved by 1% of the time
where the time goes in v6:
time: 59.2 us; the launch traced here: 58.9 us
  Pallas kernels  58.3 us (98%)
  between operations  0.64 us (1%)
    pallas_call x1, Pallas kernels, per_device(): pl.pallas_call(kernel, out_shape=(jax.ShapeDtypeStruct((DEV * PITCH, 128)...  52.1 us
    pallas_call x1, Pallas kernels, per_device(): pl.pallas_call(restore_kernel, out_shape=(jax.ShapeDtypeStruct((R, ROWS),...  6.24 us

profile of v6, /device:TPU:1, one launch (start us, length us, event | category | flops | bytes accessed | tf_op | source)
XLA Modules:
  0.0 58.9 jit_solution(14630148950275079020)
XLA Ops:
  0.6 52.1 %gmrf_solve.1 = (f32[2048,128]{1,0:T(8,128)}, s32[24,128]{1,0:T(8,128)}, f32[64,256]{1,0:T(8,128)}) custom-call(f32[64,3072]{1,0:T(8,128)} %bitcast.18, s32[24,128]{1,0:T(8,128)} %bitcast.22, f32[64,256]{1,0:T(8,128)} %bitcast.21, f32[256,256]{1,0:T(8,128)} %bitcast.19, f32[256,256]{1,0:T(8,128)} %bitcast.20, f32[12,256,256]{2,1,0:T(8,128)} %bitcast.17, ...), custom_call_target="tpu_custom_call" | custom-call | tf_op jit(solution)/shard_map/gmrf_solve/pallas_call | solution.py:637
  52.7 6.2 %restore_rows.1 = (f32[64,3072]{1,0:T(8,128)}, f32[64,256]{1,0:T(8,128)}) custom-call(f32[2048,128]{1,0:T(8,128)} %get-tuple-element.7.came_hbm, s32[24,128]{1,0:T(8,128)} %get-tuple-element.8.pos, f32[64,256]{1,0:T(8,128)} %get-tuple-element.9.sep_hbm), custom_call_target="tpu_custom_call" | custom-call | tf_op jit(solution)/shard_map/restore_rows/pallas_call | solution.py:707
